TPU v7x, 512 devices: a whole 4x4x16 slice. The times are simulated.
512 devices in a mesh: dp: 8 (over x, core), tm: 16 (over z), space: 4 (over y).
Axes of the slice: x: 4, y: 4, z: 16, core: 2. Of those that a mesh axis runs over, the one named last changes fastest.
Arguments:
- groups: bfloat16 [512, 1, 96, 16, 128], P(('dp', 'tm'), None, None, 'space'), may hold values from -6 to 6
- plan_owner: int32 [8, 64], P('dp'), may hold values from 0 to 15, as said below
- plan_slot: int32 [8, 64], P('dp'), may hold values from 0 to 3, as said below
- clip_lengths: int32 [12], replicated, may hold values from 1 to 81, 512 in all
- gain_one: float32 [96], replicated, may hold values from 0.25 to 1.75
- weight_one: bfloat16 [3, 3, 3, 96, 96], replicated, may hold values from -0.125 to 0.125
- bias_one: float32 [96], replicated, may hold values from -3 to 3
- gain_two: float32 [96], replicated, may hold values from 0.25 to 1.75
- weight_two: bfloat16 [3, 3, 3, 96, 96], replicated, may hold values from -0.125 to 0.125
- bias_two: float32 [96], replicated, may hold values from -2 to 2
Outputs:
- encoded: bfloat16 [512, 96, 16, 128], P(('dp', 'tm'), None, 'space')
Inputs may be any that keep to these rules, and one draw needn't show every extreme that they name: `plan_owner`: in each span every loader (index l along tm, entries l * 4 to l * 4 + 3) sends either none or exactly 1 of its groups to an owner, and every owner receives 4 groups. Within a span the pairs (plan_owner, plan_slot) of its groups are all different. `clip_lengths`: the lengths sum to 512; a clip may be as short as one frame.
All inputs are finite; a program needn't handle non-finite values.
Results may differ from a plain program's by a relative error of at most 0.0037.
Values may be sent and summed in bfloat16 or wider, within the bound.
A program may use at most 64 MiB of HBM per device.

v0:
```python
import jax
import jax.numpy as jnp
from jax import lax
from jax.sharding import PartitionSpec as P


def shifted(value, axis, steps):
    count = lax.axis_size(axis)
    initial, last = (max(0, -steps), min(count, count - steps))
    return lax.ppermute(value, axis, [(source, source + steps) for source in range(initial, last)])


def with_halo(block, sides, width):
    for axis, dim in sides:
        count = lax.axis_size(axis)
        forward = [(i, i + 1) for i in range(count - 1)]
        backward = [(target, source) for source, target in forward]
        low = lax.ppermute(
            lax.slice_in_dim(block, block.shape[dim] - width, None, axis=dim), axis, forward
        )
        high = lax.ppermute(lax.slice_in_dim(block, 0, width, axis=dim), axis, backward)
        block = jnp.concatenate([low, block, high], axis=dim)
    return block


def normed_silu(values, gain):
    square = jnp.mean(values * values, axis=1, keepdims=True)
    return jax.nn.silu(values * lax.rsqrt(square + 1e-06) * gain[None, :, None, None])


def frame_offsets(frame_ids, clip_lengths):
    starts = jnp.cumsum(clip_lengths) - clip_lengths
    below = starts[None, :] <= frame_ids[:, None]
    latest = jnp.max(jnp.where(below, starts[None, :], 0), axis=1)
    return frame_ids - latest


def causal_conv(field, weight, keep):
    frames = field.shape[0] - 2
    width = field.shape[1]
    rows = field.shape[2] - 2
    cols = field.shape[3]
    padded = jnp.pad(field, ((0, 0), (0, 0), (0, 0), (1, 1)))
    layers = [
        padded[tap : tap + frames] * keep[:, 2 - tap][:, None, None, None] for tap in range(3)
    ]
    stacked = jnp.stack(layers, axis=1).reshape(frames, 3 * width, rows + 2, cols + 2)
    kernel = jnp.transpose(weight, (1, 2, 3, 0, 4)).reshape(3, 3, width, 3 * width)
    total = jnp.zeros((frames, width, rows, cols), jnp.float32)
    for drow in range(3):
        for dcol in range(3):
            window = stacked[:, :, drow : drow + rows, dcol : dcol + cols]
            total = total + jnp.einsum(
                "ok,fkrw->forw", kernel[drow, dcol], window, preferred_element_type=jnp.float32
            )
    return total


def body(
    groups,
    plan_owner,
    plan_slot,
    clip_lengths,
    gain_one,
    weight_one,
    bias_one,
    gain_two,
    weight_two,
    bias_two,
):
    owners_count = lax.axis_size("tm")
    place = lax.axis_index("tm")
    span_index = lax.axis_index("dp")
    per_dev = groups.shape[0]
    capacity = max(1, per_dev // owners_count)
    frames = per_dev * groups.shape[1]
    width = groups.shape[2]
    rows = groups.shape[3]
    cols = groups.shape[4]
    owners_all = plan_owner[0].reshape(owners_count, per_dev)
    slots_all = plan_slot[0].reshape(owners_count, per_dev)
    earlier = jnp.arange(per_dev)[:, None] > jnp.arange(per_dev)[None, :]
    same_owner = owners_all[:, :, None] == owners_all[:, None, :]
    ranks = jnp.sum(same_owner & earlier[None], axis=2)
    mine_owner = lax.dynamic_index_in_dim(owners_all, place, 0, keepdims=False)
    mine_rank = lax.dynamic_index_in_dim(ranks, place, 0, keepdims=False)
    targets = jnp.arange(owners_count, dtype=jnp.int32)[:, None, None]
    copies = jnp.arange(capacity, dtype=jnp.int32)[None, :, None]
    select = (mine_owner[None, None, :] == targets) & (mine_rank[None, None, :] == copies)
    select = select.astype(jnp.bfloat16).reshape(owners_count * capacity, per_dev)
    outgoing = jnp.dot(select, groups.reshape(per_dev, -1), preferred_element_type=jnp.float32)
    outgoing = outgoing.astype(jnp.bfloat16).reshape((owners_count * capacity,) + groups.shape[1:])
    incoming = lax.all_to_all(outgoing, "tm", split_axis=0, concat_axis=0, tiled=True)
    slot_ids = jnp.arange(per_dev, dtype=jnp.int32)[:, None, None, None]
    copy_ids = jnp.arange(capacity, dtype=jnp.int32)[None, None, :, None]
    pick = (
        (owners_all == place)[None, :, None, :]
        & (slots_all[None, :, None, :] == slot_ids)
        & (ranks[None, :, None, :] == copy_ids)
    )
    pick = (
        jnp.sum(pick.astype(jnp.int32), axis=3)
        .astype(jnp.bfloat16)
        .reshape(per_dev, owners_count * capacity)
    )
    local = jnp.dot(
        pick, incoming.reshape(owners_count * capacity, -1), preferred_element_type=jnp.float32
    )
    local = local.astype(jnp.bfloat16).reshape(frames, width, rows, cols)
    first = (span_index * owners_count + place) * frames
    frame_ids = first - 4 + jnp.arange(frames + 4, dtype=jnp.int32)
    offsets = frame_offsets(frame_ids, clip_lengths)
    keep = (offsets[:, None] >= jnp.arange(3, dtype=jnp.int32)[None, :]).astype(jnp.bfloat16)
    residual = local.astype(jnp.float32)
    hidden_one = normed_silu(residual, gain_one).astype(jnp.bfloat16)
    cache_first = shifted(hidden_one[frames - 2 :], ("dp", "tm"), 1)
    banded_one = with_halo(jnp.concatenate([cache_first, hidden_one], axis=0), (("space", 2),), 1)
    act = causal_conv(banded_one, weight_one, keep[4:]) + bias_one[None, :, None, None]
    hidden_two = normed_silu(act, gain_two).astype(jnp.bfloat16)
    cache_second = shifted(hidden_two[frames - 2 :], ("dp", "tm"), 1)
    banded_two = with_halo(jnp.concatenate([cache_second, hidden_two], axis=0), (("space", 2),), 1)
    mixed = causal_conv(banded_two, weight_two, keep[4:])
    return (residual + mixed + bias_two[None, :, None, None]).astype(jnp.bfloat16)


def solution(mesh):
    return jax.shard_map(
        body,
        mesh=mesh,
        in_specs=(
            P(("dp", "tm"), None, None, "space", None),
            P("dp", None),
            P("dp", None),
            P(),
            P(),
            P(),
            P(),
            P(),
            P(),
            P(),
        ),
        out_specs=P(("dp", "tm"), None, "space", None),
        check_vma=False,
    )
```

profile of v0, /device:TPU:6, one launch (start us, length us, event | category | flops | bytes accessed | tf_op | source)
XLA Modules:
  0.0 158.5 jit_solution(4383610414670553931)
XLA Ops:
  0.5 1.3 reduce.10
  2.3 1.1 reshape.226
  4.2 2.2 %reshape.227 = bf16[16,1,96,4,128]{4,3,2,0,1:T(4,128)(2,1)} reshape(bf16[16,49152]{1,0:T(8,128)(2,1)S(1)} %convolution_convert_fusion) | data formatting | bytes 3145728 | tf_op jit(solution)/shard_map/reshape | solution.py:92
  6.4 15.3 %all-to-all-start = ((bf16[16,1,96,4,128]{4,3,2,1,0:T(4,128)(2,1)}), bf16[16,1,96,4,128]{4,3,2,1,0:T(4,128)(2,1)S(1)}, u32[]{:S(2)}, u32[]{:S(2)}) async-start(bf16[16,1,96,4,128]{4,3,2,1,0:T(4,128)(2,1)} %bitcast.2), calls=%async_computation | async-start | bytes 3145728 | tf_op jit(solution)/shard_map/all_to_all | solution.py:93
  22.8 1.1 copy.93
  24.2 71.8 %all-to-all-done = bf16[16,1,96,4,128]{4,3,2,1,0:T(4,128)(2,1)S(1)} async-done(((bf16[16,1,96,4,128]{4,3,2,1,0:T(4,128)(2,1)}), bf16[16,1,96,4,128]{4,3,2,1,0:T(4,128)(2,1)S(1)}, u32[]{:S(2)}, u32[]{:S(2)}) %all-to-all-start) | async-done | bytes 1572896 | tf_op jit(solution)/shard_map/all_to_all | solution.py:93
  96.0 1.2 reshape.228
  98.8 2.3 %collective-permute-start = (bf16[2,96,4,128]{3,1,2,0:T(8,128)(2,1)S(1)}, bf16[2,96,4,128]{3,1,2,0:T(8,128)(2,1)S(1)}, u32[]{:S(2)}, u32[]{:S(2)}) collective-permute-start(bf16[2,96,4,128]{3,1,2,0:T(8,128)(2,1)S(1)} %slice.214), channel_id=1, source_target_pairs={{0,4},{4,8},{8,12},{12,16},{16,20},{20,24},{24,28},{28,32},{32,36}... | collective-permute-start | bytes 589832 | tf_op jit(solution)/shard_map/ppermute | solution.py:10
  101.1 8.7 %collective-permute-done = bf16[2,96,4,128]{3,1,2,0:T(8,128)(2,1)S(1)} collective-permute-done((bf16[2,96,4,128]{3,1,2,0:T(8,128)(2,1)S(1)}, bf16[2,96,4,128]{3,1,2,0:T(8,128)(2,1)S(1)}, u32[]{:S(2)}, u32[]{:S(2)}) %collective-permute-start) | collective-permute-done | bytes 196640 | tf_op jit(solution)/shard_map/ppermute | solution.py:10
  109.8 3.5 %collective-permute-start.1 = (bf16[6,96,1,128]{3,1,2,0:T(8,128)(2,1)S(1)}, bf16[6,96,1,128]{3,1,2,0:T(8,128)(2,1)S(1)}, u32[]{:S(2)}, u32[]{:S(2)}) collective-permute-start(bf16[6,96,1,128]{3,1,2,0:T(8,128)(2,1)S(1)} %get-tuple-element.13), channel_id=1, source_target_pairs={{0,1},{1,2},{2,3},{4,5},{5,6},{6,7},{8,9},{9,10},{10,11},{12,13},{... | collective-permute-start | bytes 442376 | tf_op jit(solution)/shard_map/ppermute | solution.py:18
  113.3 1.3 collective-permute-start.2
  114.7 1.3 collective-permute-done.1
  115.9 4.4 %collective-permute-done.2 = bf16[6,96,1,128]{3,1,2,0:T(8,128)(2,1)S(1)} collective-permute-done((bf16[6,96,1,128]{3,1,2,0:T(8,128)(2,1)S(1)}, bf16[6,96,1,128]{3,1,2,0:T(8,128)(2,1)S(1)}, u32[]{:S(2)}, u32[]{:S(2)}) %collective-permute-start.2) | collective-permute-done | bytes 147488 | tf_op jit(solution)/shard_map/ppermute | solution.py:21
  120.3 1.0 fusion.9
  121.6 0.8 pad_maximum_fusion
  129.3 1.9 %collective-permute-start.3 = (bf16[2,96,4,128]{3,1,2,0:T(8,128)(2,1)S(1)}, bf16[2,96,4,128]{3,1,2,0:T(8,128)(2,1)S(1)}, u32[]{:S(2)}, u32[]{:S(2)}) collective-permute-start(bf16[2,96,4,128]{3,1,2,0:T(8,128)(2,1)S(1)} %slice.235), channel_id=1, source_target_pairs={{0,4},{4,8},{8,12},{12,16},{16,20},{20,24},{24,28},{28,32},{32,36}... | collective-permute-start | bytes 589832 | tf_op jit(solution)/shard_map/ppermute | solution.py:10
  131.2 8.0 %collective-permute-done.3 = bf16[2,96,4,128]{3,1,2,0:T(8,128)(2,1)S(1)} collective-permute-done((bf16[2,96,4,128]{3,1,2,0:T(8,128)(2,1)S(1)}, bf16[2,96,4,128]{3,1,2,0:T(8,128)(2,1)S(1)}, u32[]{:S(2)}, u32[]{:S(2)}) %collective-permute-start.3) | collective-permute-done | bytes 196640 | tf_op jit(solution)/shard_map/ppermute | solution.py:10
  139.2 3.5 %collective-permute-start.4 = (bf16[6,96,1,128]{3,1,2,0:T(8,128)(2,1)S(1)}, bf16[6,96,1,128]{3,1,2,0:T(8,128)(2,1)S(1)}, u32[]{:S(2)}, u32[]{:S(2)}) collective-permute-start(bf16[6,96,1,128]{3,1,2,0:T(8,128)(2,1)S(1)} %get-tuple-element.11), channel_id=1, source_target_pairs={{0,1},{1,2},{2,3},{4,5},{5,6},{6,7},{8,9},{9,10},{10,11},{12,13},{... | collective-permute-start | bytes 442376 | tf_op jit(solution)/shard_map/ppermute | solution.py:18
  142.7 1.5 collective-permute-start.5
  144.5 0.8 collective-permute-done.4
  145.4 4.4 %collective-permute-done.5 = bf16[6,96,1,128]{3,1,2,0:T(8,128)(2,1)S(1)} collective-permute-done((bf16[6,96,1,128]{3,1,2,0:T(8,128)(2,1)S(1)}, bf16[6,96,1,128]{3,1,2,0:T(8,128)(2,1)S(1)}, u32[]{:S(2)}, u32[]{:S(2)}) %collective-permute-start.5) | collective-permute-done | bytes 147488 | tf_op jit(solution)/shard_map/ppermute | solution.py:21
  149.7 1.0 select_maximum_fusion
  151.0 0.8 pad_maximum_fusion.1
  157.5 0.9 copy.124
  (74 shorter events, 17.9 us)
Async XLA Ops:
  6.4 15.5 %copy-start.7 = (s32[1,64]{1,0:T(1,128)S(1)}, s32[1,64]{1,0:T(1,128)}, u32[]{:S(2)}) copy-start(s32[1,64]{1,0:T(1,128)} %param.12) | copy-start | bytes 772
  6.4 16.3 %copy-start.8 = (s32[12]{0:T(128)S(1)}, s32[12]{0:T(128)}, u32[]{:S(2)}) copy-start(s32[12]{0:T(128)} %param.13) | copy-start | bytes 148
  6.4 16.5 %copy-start.1 = (bf16[3,3,3,96,96]{4,3,2,1,0:T(8,128)(2,1)S(1)}, bf16[3,3,3,96,96]{4,3,2,1,0:T(8,128)(2,1)}, u32[]{:S(2)}) copy-start(bf16[3,3,3,96,96]{4,3,2,1,0:T(8,128)(2,1)} %param.15) | copy-start | bytes 1492996
  6.4 89.6 %all-to-all-start = ((bf16[16,1,96,4,128]{4,3,2,1,0:T(4,128)(2,1)}), bf16[16,1,96,4,128]{4,3,2,1,0:T(4,128)(2,1)S(1)}, u32[]{:S(2)}, u32[]{:S(2)}) async-start(bf16[16,1,96,4,128]{4,3,2,1,0:T(4,128)(2,1)} %bitcast.2), calls=%async_computation | async-start | bytes 3145728 | tf_op jit(solution)/shard_map/all_to_all | solution.py:93
  97.6 0.9 copy-start.3
  98.8 11.0 %collective-permute-start = (bf16[2,96,4,128]{3,1,2,0:T(8,128)(2,1)S(1)}, bf16[2,96,4,128]{3,1,2,0:T(8,128)(2,1)S(1)}, u32[]{:S(2)}, u32[]{:S(2)}) collective-permute-start(bf16[2,96,4,128]{3,1,2,0:T(8,128)(2,1)S(1)} %slice.214), channel_id=1, source_target_pairs={{0,4},{4,8},{8,12},{12,16},{16,20},{20,24},{24,28},{28,32},{32,36}... | collective-permute-start | bytes 589832 | tf_op jit(solution)/shard_map/ppermute | solution.py:10
  109.8 6.2 %collective-permute-start.1 = (bf16[6,96,1,128]{3,1,2,0:T(8,128)(2,1)S(1)}, bf16[6,96,1,128]{3,1,2,0:T(8,128)(2,1)S(1)}, u32[]{:S(2)}, u32[]{:S(2)}) collective-permute-start(bf16[6,96,1,128]{3,1,2,0:T(8,128)(2,1)S(1)} %get-tuple-element.13), channel_id=1, source_target_pairs={{0,1},{1,2},{2,3},{4,5},{5,6},{6,7},{8,9},{9,10},{10,11},{12,13},{... | collective-permute-start | bytes 442376 | tf_op jit(solution)/shard_map/ppermute | solution.py:18
  113.3 7.0 %collective-permute-start.2 = (bf16[6,96,1,128]{3,1,2,0:T(8,128)(2,1)S(1)}, bf16[6,96,1,128]{3,1,2,0:T(8,128)(2,1)S(1)}, u32[]{:S(2)}, u32[]{:S(2)}) collective-permute-start(bf16[6,96,1,128]{3,1,2,0:T(8,128)(2,1)S(1)} %get-tuple-element.14), channel_id=1, source_target_pairs={{1,0},{2,1},{3,2},{5,4},{6,5},{7,6},{9,8},{10,9},{11,10},{13,12},{... | collective-permute-start | bytes 442376 | tf_op jit(solution)/shard_map/ppermute | solution.py:21
  122.5 1.1 copy-start
  127.5 0.7 copy-start.4
  128.2 0.7 copy-start.5
  128.9 15.3 %copy-start.2 = (bf16[3,3,3,96,96]{4,3,2,1,0:T(8,128)(2,1)S(1)}, bf16[3,3,3,96,96]{4,3,2,1,0:T(8,128)(2,1)}, u32[]{:S(2)}) copy-start(bf16[3,3,3,96,96]{4,3,2,1,0:T(8,128)(2,1)} %param.18) | copy-start | bytes 1492996
  129.3 9.9 %collective-permute-start.3 = (bf16[2,96,4,128]{3,1,2,0:T(8,128)(2,1)S(1)}, bf16[2,96,4,128]{3,1,2,0:T(8,128)(2,1)S(1)}, u32[]{:S(2)}, u32[]{:S(2)}) collective-permute-start(bf16[2,96,4,128]{3,1,2,0:T(8,128)(2,1)S(1)} %slice.235), channel_id=1, source_target_pairs={{0,4},{4,8},{8,12},{12,16},{16,20},{20,24},{24,28},{28,32},{32,36}... | collective-permute-start | bytes 589832 | tf_op jit(solution)/shard_map/ppermute | solution.py:10
  139.2 6.1 %collective-permute-start.4 = (bf16[6,96,1,128]{3,1,2,0:T(8,128)(2,1)S(1)}, bf16[6,96,1,128]{3,1,2,0:T(8,128)(2,1)S(1)}, u32[]{:S(2)}, u32[]{:S(2)}) collective-permute-start(bf16[6,96,1,128]{3,1,2,0:T(8,128)(2,1)S(1)} %get-tuple-element.11), channel_id=1, source_target_pairs={{0,1},{1,2},{2,3},{4,5},{5,6},{6,7},{8,9},{9,10},{10,11},{12,13},{... | collective-permute-start | bytes 442376 | tf_op jit(solution)/shard_map/ppermute | solution.py:18
  142.7 7.0 %collective-permute-start.5 = (bf16[6,96,1,128]{3,1,2,0:T(8,128)(2,1)S(1)}, bf16[6,96,1,128]{3,1,2,0:T(8,128)(2,1)S(1)}, u32[]{:S(2)}, u32[]{:S(2)}) collective-permute-start(bf16[6,96,1,128]{3,1,2,0:T(8,128)(2,1)S(1)} %get-tuple-element.12), channel_id=1, source_target_pairs={{1,0},{2,1},{3,2},{5,4},{6,5},{7,6},{9,8},{10,9},{11,10},{13,12},{... | collective-permute-start | bytes 442376 | tf_op jit(solution)/shard_map/ppermute | solution.py:21
  156.2 0.7 copy-start.6
where the time goes:
time: 159 us; the launch traced here: 158 us
  waiting for transfers between devices  99.3 us (62%)
  starting transfers between devices  29.3 us (18%)
  matrix products  11.7 us (7%)
  local copies, waits for them, and re-layouts  10 us (6%)
  other arithmetic  7.76 us (5%)
    all_to_all x1, waiting for transfers between devices, body(): lax.all_to_all(outgoing, 'tm', split_axis=0, concat_axis=0, tiled=True)  71.8 us
    ppermute x2, waiting for transfers between devices, shifted(): lax.ppermute(value, axis, [(source, source + steps) for source in range(i...  16.7 us
    all_to_all x1, starting transfers between devices, body(): lax.all_to_all(outgoing, 'tm', split_axis=0, concat_axis=0, tiled=True)  15.3 us
    dot_general x18, matrix products, causal_conv(): jnp.einsum('ok,fkrw->forw', kernel[drow, dcol], window, preferred_element...  10.6 us
    ppermute x2, waiting for transfers between devices, with_halo(): lax.ppermute(lax.slice_in_dim(block, 0, width, axis=dim), axis, backward)  8.77 us
    ppermute x2, starting transfers between devices, with_halo(): lax.ppermute(lax.slice_in_dim(block, block.shape[dim] - width, None, axis...  6.96 us
    ppermute x2, starting transfers between devices, shifted(): lax.ppermute(value, axis, [(source, source + steps) for source in range(i...  4.2 us
  transfers between devices with their start and end apart: 7, of which 7 were waited for; matrix products, arithmetic and copies ran while one was open for 2% of the time, Pallas kernels for 0%

commit v1 on v0

--- a/solution.py
+++ b/solution.py
@@ -1,7 +1,13 @@
 import jax
 import jax.numpy as jnp
 from jax import lax
+from jax.experimental import pallas as pl
+from jax.experimental.pallas import tpu as pltpu
 from jax.sharding import PartitionSpec as P
+
+MESH = pl.DeviceIdType.MESH
+STEPS = 14
+PARTS = 2
 
 
 def shifted(value, axis, steps):
@@ -56,7 +62,7 @@
     return total
 
 
-def body(
+def general_body(
     groups,
     plan_owner,
     plan_slot,
@@ -123,6 +129,275 @@
     return (residual + mixed + bias_two[None, :, None, None]).astype(jnp.bfloat16)
 
 
+def column(row, size):
+    down = lax.broadcasted_iota(jnp.int32, (size, size), 0)
+    across = lax.broadcasted_iota(jnp.int32, (size, size), 1)
+    spread = jnp.where(down == across, jnp.broadcast_to(row, (size, size)), jnp.zeros((), row.dtype))
+    return jnp.sum(spread, axis=1, keepdims=True)
+
+
+def plan_schedule(owner_ref, slot_ref, sched, count, per_dev):
+    total = count * per_dev
+    shape = (total, 128)
+    frame = lax.broadcasted_iota(jnp.int32, shape, 0)
+    lane = lax.broadcasted_iota(jnp.int32, shape, 1) & (count - 1)
+    owner = jnp.broadcast_to(column(owner_ref[...], total), shape)
+    place = jnp.broadcast_to(column(slot_ref[...], total), shape)
+    source = frame // per_dev
+    entry = frame - source * per_dev
+    ahead = (owner - source) & (count - 1)
+    half = count // 2
+    forward = (ahead < half) | ((ahead == half) & ((source & 1) == 0))
+    here = lane == source
+    code = (frame << 10) | (place << 8) | entry
+    right = jnp.where(here & forward & (ahead > 0), (ahead << 16) | code, 0)
+    left = jnp.where(here & jnp.logical_not(forward), ((count - ahead) << 16) | code, 0)
+    final = tuple(
+        jnp.max(jnp.where(here & (ahead == 0) & (place == s), entry, 0), axis=0, keepdims=True)
+        for s in range(per_dev)
+    )
+
+    def one(t, way, state, final):
+        best = jnp.max(state, axis=0, keepdims=True)
+        sched[pl.ds(2 * t + way, 1), :] = best & 255
+        state = jnp.where(state == best, 0, state)
+        entry = per_dev + 2 * t + way
+        moved = jnp.where(best > 0, best - (best & 255) - (1 << 16) + entry, -1)
+        moved = pltpu.roll(moved, 1 if way == 0 else 127, 1)
+        there = (moved >= 0) & (moved < (1 << 16))
+        final = tuple(
+            jnp.where(there & (((moved >> 8) & 3) == s), entry, final[s]) for s in range(per_dev)
+        )
+        state = jnp.where((frame == ((moved >> 10) & 63)) & (moved >= (1 << 16)), moved, state)
+        return state, final
+
+    def step(t, carry):
+        right, left, final = carry
+        right, final = one(t, 0, right, final)
+        left, final = one(t, 1, left, final)
+        return right, left, final
+
+    right, left, final = lax.fori_loop(0, STEPS, step, (right, left, final))
+    for s in range(per_dev):
+        sched[pl.ds(2 * STEPS + s, 1), :] = final[s]
+    late = jnp.max(jnp.maximum(right, left), axis=0, keepdims=True)
+    late = jnp.max(late, axis=1, keepdims=True)
+    return (late > 0).astype(jnp.float32)
+
+
+def silu_norm(values, gain):
+    square = jnp.mean(values * values, axis=0, keepdims=True)
+    scaled = values * lax.rsqrt(square + 1e-06) * gain
+    return scaled / (1.0 + jnp.exp(-scaled))
+
+
+def conv_rows(field, weights, mask, at, rows):
+    ch, cols = field.shape[2], field.shape[3]
+    right_side = jnp.concatenate(
+        [field[at : at + 3, r : r + 3].reshape(9 * ch, cols) for r in range(rows)], axis=1
+    )
+    sums = jnp.dot(weights * mask, right_side, preferred_element_type=jnp.float32)
+    lane = lax.broadcasted_iota(jnp.int32, (ch, cols), 1)
+    out = []
+    for r in range(rows):
+        part = sums[:, r * cols : (r + 1) * cols]
+        low = jnp.where(lane == 0, 0.0, pltpu.roll(part[:ch], 1, 1))
+        high = jnp.where(lane == cols - 1, 0.0, pltpu.roll(part[2 * ch :], cols - 1, 1))
+        out.append(part[ch : 2 * ch] + low + high)
+    return out
+
+
+def block_kernel(
+    groups, owner, slot, clips, gain_one, weight_one, bias_one, gain_two, weight_two, bias_two,
+    out, late_out,
+    pool, sending, arrived, sched, sched_s, h_one, h_two, timeline, late_all,
+    send_sem, recv_sem, sched_sem, halo_send, halo_recv, late_send, late_recv,
+):
+    spans, places, bands = lax.axis_size("dp"), lax.axis_size("tm"), lax.axis_size("space")
+    dp, tm, sp = lax.axis_index("dp"), lax.axis_index("tm"), lax.axis_index("space")
+    per_dev, rows, ch, cols = out.shape
+    part_rows = rows * ch // PARTS
+    tm_up, tm_down = lax.rem(tm + 1, places), lax.rem(tm + places - 1, places)
+    sp_up, sp_down = lax.rem(sp + 1, bands), lax.rem(sp + bands - 1, bands)
+    dp_up, dp_down = lax.rem(dp + 1, spans), lax.rem(dp + spans - 1, spans)
+    dp_next = jnp.where(tm == places - 1, dp_up, dp)
+    dp_prev = jnp.where(tm == 0, dp_down, dp)
+
+    barrier = pltpu.get_barrier_semaphore()
+    friends = [(dp, tm_up, sp), (dp, tm_down, sp), (dp, tm, sp_up), (dp, tm, sp_down)]
+    friends += [(dp_next, tm_up, s) for s in (sp, sp_up, sp_down)]
+    friends += [(dp_prev, tm_down, s) for s in (sp, sp_up, sp_down)]
+    friends += [(lax.rem(dp + k, spans), tm, sp) for k in range(1, 8)]
+    for friend in friends:
+        pl.semaphore_signal(barrier, inc=1, device_id=friend, device_id_type=MESH)
+
+    late = plan_schedule(owner, slot, sched, places, per_dev)
+    late_all[0] = jnp.broadcast_to(late, (8, 128))
+    to_scalars = pltpu.make_async_copy(sched, sched_s, sched_sem)
+    to_scalars.start()
+    for f in range(per_dev):
+        for p in range(PARTS):
+            pool[f, p] = groups[f, p * part_rows : (p + 1) * part_rows]
+    to_scalars.wait()
+    pl.semaphore_wait(barrier, len(friends))
+
+    late_copies = []
+    for k in range(1, 8):
+        copy = pltpu.make_async_remote_copy(
+            src_ref=late_all.at[0], dst_ref=late_all.at[k], send_sem=late_send.at[k - 1],
+            recv_sem=late_recv.at[k - 1], device_id=(lax.rem(dp + k, spans), tm, sp), device_id_type=MESH,
+        )
+        copy.start()
+        late_copies.append(copy)
+
+    def hop(t, way, p):
+        return pltpu.make_async_remote_copy(
+            src_ref=sending.at[t, way, p], dst_ref=arrived.at[t, way, p],
+            send_sem=send_sem.at[t, way, p], recv_sem=recv_sem.at[t, way, p],
+            device_id=(dp, tm_up if way == 0 else tm_down, sp), device_id_type=MESH,
+        )
+
+    def send(t, p):
+        for way in range(2):
+            sending[t, way, p] = pool[sched_s[2 * t + way, tm], p]
+            hop(t, way, p).start()
+
+    def receive(t, p):
+        for way in range(2):
+            hop(t, way, p).wait()
+            pool[per_dev + 2 * t + way, p] = arrived[t, way, p]
+
+    for p in range(PARTS):
+        send(0, p)
+
+    def step(t, carry):
+        for p in range(PARTS):
+            receive(t - 1, p)
+            send(t, p)
+        return carry
+
+    lax.fori_loop(1, STEPS, step, 0)
+    for p in range(PARTS):
+        receive(STEPS - 1, p)
+
+    gain_a = column(gain_one[...], ch)
+    gain_b = column(gain_two[...], ch)
+    bias_a = column(bias_one[...], ch)
+    bias_b = column(bias_two[...], ch)
+    first = (dp * places + tm) * per_dev
+    offsets = []
+    for s in range(per_dev):
+        start, latest = jnp.int32(0), jnp.int32(0)
+        for c in range(clips.shape[1]):
+            latest = jnp.where(start <= first + s, start, latest)
+            start = start + clips[0, c]
+        offsets.append(first + s - latest)
+    tap = lax.broadcasted_iota(jnp.int32, (1, 9 * ch), 1) // (3 * ch)
+    masks = [(2 - tap <= offsets[s]).astype(jnp.float32).astype(jnp.bfloat16) for s in range(per_dev)]
+
+    for s in range(per_dev):
+        entry = sched_s[2 * STEPS + s, tm]
+        for p in range(PARTS):
+            timeline[s, p] = pool[entry, p]
+        for r in range(rows):
+            p, at = divmod(r * ch, part_rows)
+            values = timeline[s, p, at : at + ch].astype(jnp.float32)
+            h_one[2 + s, 1 + r] = silu_norm(values, gain_a).astype(jnp.bfloat16)
+
+    def exchange(field, turn):
+        copies = []
+        for k, (src, dst, device) in enumerate((
+            (field.at[4:6, 1:5], field.at[0:2, 1:5], (dp_next, tm_up, sp)),
+            (field.at[2:6, 4], field.at[2:6, 0], (dp, tm, sp_up)),
+            (field.at[2:6, 1], field.at[2:6, 5], (dp, tm, sp_down)),
+            (field.at[4:6, 4], field.at[0:2, 0], (dp_next, tm_up, sp_up)),
+            (field.at[4:6, 1], field.at[0:2, 5], (dp_next, tm_up, sp_down)),
+        )):
+            copy = pltpu.make_async_remote_copy(
+                src_ref=src, dst_ref=dst, send_sem=halo_send.at[turn, k], recv_sem=halo_recv.at[turn, k],
+                device_id=device, device_id_type=MESH,
+            )
+            copy.start()
+            copies.append(copy)
+        for copy in copies:
+            copy.wait()
+
+        @pl.when(sp == 0)
+        def _():
+            field[:, 0] = jnp.zeros((per_dev + 2, ch, cols), field.dtype)
+
+        @pl.when(sp == bands - 1)
+        def _():
+            field[:, rows + 1] = jnp.zeros((per_dev + 2, ch, cols), field.dtype)
+
+    exchange(h_one, 0)
+    for s in range(per_dev):
+        for r, act in enumerate(conv_rows(h_one, weight_one[...], masks[s], s, rows)):
+            h_two[2 + s, 1 + r] = silu_norm(act + bias_a, gain_b).astype(jnp.bfloat16)
+    exchange(h_two, 1)
+    for s in range(per_dev):
+        for r, mixed in enumerate(conv_rows(h_two, weight_two[...], masks[s], s, rows)):
+            p, at = divmod(r * ch, part_rows)
+            kept = timeline[s, p, at : at + ch].astype(jnp.float32)
+            out[s, r] = (kept + mixed + bias_b).astype(jnp.bfloat16)
+
+    for copy in late_copies:
+        copy.wait()
+    late_out[...] = jnp.max(late_all[...], axis=0)
+
+
+def body(
+    groups, plan_owner, plan_slot, clip_lengths, gain_one, weight_one, bias_one, gain_two, weight_two, bias_two
+):
+    per_dev, _, ch, rows, cols = groups.shape
+    turned = jnp.transpose(groups[:, 0], (0, 2, 1, 3)).reshape(per_dev, rows * ch, cols)
+    weights = [
+        jnp.transpose(w, (2, 3, 0, 1, 4)).reshape(3 * ch, 9 * ch) for w in (weight_one, weight_two)
+    ]
+    vmem, smem = pl.BlockSpec(memory_space=pltpu.VMEM), pl.BlockSpec(memory_space=pltpu.SMEM)
+    part = (PARTS, rows * ch // PARTS, cols)
+    sched_rows = (2 * STEPS + per_dev + 7) // 8 * 8
+    fast, late = pl.pallas_call(
+        block_kernel,
+        out_shape=(
+            jax.ShapeDtypeStruct((per_dev, rows, ch, cols), jnp.bfloat16),
+            jax.ShapeDtypeStruct((8, 128), jnp.float32),
+        ),
+        in_specs=[vmem, vmem, vmem, smem] + [vmem] * 6,
+        out_specs=(vmem, vmem),
+        scratch_shapes=[
+            pltpu.VMEM((per_dev + 2 * STEPS,) + part, jnp.bfloat16),
+            pltpu.VMEM((STEPS, 2) + part, jnp.bfloat16),
+            pltpu.VMEM((STEPS, 2) + part, jnp.bfloat16),
+            pltpu.VMEM((sched_rows, 128), jnp.int32),
+            pltpu.SMEM((sched_rows, 128), jnp.int32),
+            pltpu.VMEM((per_dev + 2, rows + 2, ch, cols), jnp.bfloat16),
+            pltpu.VMEM((per_dev + 2, rows + 2, ch, cols), jnp.bfloat16),
+            pltpu.VMEM((per_dev,) + part, jnp.bfloat16),
+            pltpu.VMEM((8, 8, 128), jnp.float32),
+            pltpu.SemaphoreType.DMA((STEPS, 2, PARTS)),
+            pltpu.SemaphoreType.DMA((STEPS, 2, PARTS)),
+            pltpu.SemaphoreType.DMA,
+            pltpu.SemaphoreType.DMA((2, 5)),
+            pltpu.SemaphoreType.DMA((2, 5)),
+            pltpu.SemaphoreType.DMA((7,)),
+            pltpu.SemaphoreType.DMA((7,)),
+        ],
+        compiler_params=pltpu.CompilerParams(
+            collective_id=0, has_side_effects=True, vmem_limit_bytes=48 * 2**20
+        ),
+    )(
+        turned, plan_owner, plan_slot, clip_lengths[None], gain_one[None], weights[0], bias_one[None],
+        gain_two[None], weights[1], bias_two[None],
+    )
+    return lax.cond(
+        late[0, 0] > 0,
+        lambda *args: general_body(*args),
+        lambda *args: jnp.transpose(fast, (0, 2, 1, 3)),
+        groups, plan_owner, plan_slot, clip_lengths, gain_one, weight_one, bias_one, gain_two, weight_two, bias_two,
+    )
+
+
 def solution(mesh):
     return jax.shard_map(
         body,

time: 159 us -> 95.5 us (0.60)
  the two profiles are of different devices: /device:TPU:6 before, /device:TPU:1 now
where the time goes in v1:
time: 95.5 us; the launch traced here: 95.4 us
  Pallas kernels  89.4 us (94%)
  local copies, waits for them, and re-layouts  4.85 us (5%)
    pallas_call x1, Pallas kernels, body(): pl.pallas_call(block_kernel, out_shape=(jax.ShapeDtypeStruct((per_dev, ro...  89.4 us
    transpose x2, local copies, waits for them, and re-layouts, body(): jnp.transpose(w, (2, 3, 0, 1, 4)).reshape(3 * ch, 9 * ch)  2.07 us

profile of v1, /device:TPU:1, one launch (start us, length us, event | category | flops | bytes accessed | tf_op | source)
XLA Modules:
  0.0 95.4 jit_solution(1318359196807957947)
XLA Ops:
  0.0 1.6 %copy.134 = bf16[3,96,3,3,96]{4,3,2,1,0:T(4,128)(2,1)S(1)} copy(bf16[3,96,3,3,96]{4,1,0,3,2:T(8,128)(2,1)} %bitcast.254) | data formatting | bytes 995328 | tf_op jit(solution)/shard_map/transpose | solution.py:355
  1.6 0.6 reshape.240.weight_one
  2.2 0.0 copy-start.4
  2.2 0.0 copy-done.2
  2.2 0.0 copy-start.6
  2.3 0.0 copy-start.7
  2.3 0.0 copy-start.8
  2.3 0.0 copy-start.9
  2.3 0.0 copy-start.10
  2.3 0.0 copy-start.11
  2.3 0.0 copy-start.12
  2.3 0.5 copy.135
  2.8 0.0 copy-start.1
  2.8 0.6 reshape.241.weight_two
  3.4 0.0 copy-done.4
  3.4 0.1 copy.133
  3.5 0.0 copy-done.6
  3.5 0.0 copy-done.7
  3.6 89.4 %shard_map.102 = (bf16[4,4,96,128]{3,2,1,0:T(8,128)(2,1)S(1)}, f32[8,128]{1,0:T(8,128)S(1)}) custom-call(bf16[4,384,128]{2,1,0:T(8,128)(2,1)S(1)} %bitcast.217, s32[1,64]{1,0:T(1,128)S(1)} %copy-done.10, s32[1,64]{1,0:T(1,128)S(1)} %copy-done.11, s32[1,12]{1,0:T(1,128)S(1)} %bitcast.262, f32[1,96]{1,0:T(1,128)S(1)} %bitcast.258, ...), custom_call_target="tpu_custom_call" | custom-call | tf_op jit(solution)/shard_map/pallas_call | solution.py:360
  93.0 0.5 slice.164
  94.2 0.4 conditional.1
  94.2 0.2 copy.157
  94.6 0.0 copy-start.5
  94.7 0.7 copy-done.5
  (7 shorter events, 0.0 us)
Async XLA Ops:
  0.0 2.2 %copy-start.2 = (bf16[3,3,3,96,96]{4,3,2,1,0:T(8,128)(2,1)S(1)}, bf16[3,3,3,96,96]{4,3,2,1,0:T(8,128)(2,1)}, u32[]{:S(2)}) copy-start(bf16[3,3,3,96,96]{4,3,2,1,0:T(8,128)(2,1)} %param.20) | copy-start | bytes 1492996
  2.2 1.2 %copy-start.4 = (bf16[4,1,96,4,128]{4,3,2,1,0:T(4,128)(2,1)S(1)}, bf16[4,1,96,4,128]{4,3,2,1,0:T(4,128)(2,1)}, u32[]{:S(2)}) copy-start(bf16[4,1,96,4,128]{4,3,2,1,0:T(4,128)(2,1)} %param.12) | copy-start | bytes 1179652
  2.2 1.2 %copy-start.6 = (f32[96]{0:T(128)S(1)}, f32[96]{0:T(128)}, u32[]{:S(2)}) copy-start(f32[96]{0:T(128)} %param.16) | copy-start | bytes 1156
  2.3 1.2 %copy-start.7 = (f32[96]{0:T(128)S(1)}, f32[96]{0:T(128)}, u32[]{:S(2)}) copy-start(f32[96]{0:T(128)} %param.18) | copy-start | bytes 1156
  2.3 1.2 %copy-start.8 = (f32[96]{0:T(128)S(1)}, f32[96]{0:T(128)}, u32[]{:S(2)}) copy-start(f32[96]{0:T(128)} %param.19) | copy-start | bytes 1156
  2.3 1.2 %copy-start.9 = (f32[96]{0:T(128)S(1)}, f32[96]{0:T(128)}, u32[]{:S(2)}) copy-start(f32[96]{0:T(128)} %param.21) | copy-start | bytes 1156
  2.3 1.2 %copy-start.10 = (s32[1,64]{1,0:T(1,128)S(1)}, s32[1,64]{1,0:T(1,128)}, u32[]{:S(2)}) copy-start(s32[1,64]{1,0:T(1,128)} %owner.1) | copy-start | bytes 772
  2.3 1.2 %copy-start.11 = (s32[1,64]{1,0:T(1,128)S(1)}, s32[1,64]{1,0:T(1,128)}, u32[]{:S(2)}) copy-start(s32[1,64]{1,0:T(1,128)} %slot.1) | copy-start | bytes 772
  2.3 1.2 %copy-start.12 = (s32[12]{0:T(128)S(1)}, s32[12]{0:T(128)}, u32[]{:S(2)}) copy-start(s32[12]{0:T(128)} %param.15) | copy-start | bytes 148
  2.8 91.4 %copy-start.1 = (bf16[3,3,3,96,96]{4,3,2,1,0:T(8,128)(2,1)S(1)}, bf16[3,3,3,96,96]{4,3,2,1,0:T(8,128)(2,1)}, u32[]{:S(2)}) copy-start(bf16[3,3,3,96,96]{4,3,2,1,0:T(8,128)(2,1)} %param.17) | copy-start | bytes 1492996
  94.6 0.7 copy-start.5

commit v2 on v0

--- a/solution.py
+++ b/solution.py
@@ -1,7 +1,14 @@
 import jax
 import jax.numpy as jnp
 from jax import lax
+from jax.experimental import pallas as pl
+from jax.experimental.pallas import tpu as pltpu
 from jax.sharding import PartitionSpec as P
+
+MESH = pl.DeviceIdType.MESH
+STEPS = 8
+LANES = 2
+PARTS = 2
 
 
 def shifted(value, axis, steps):
@@ -56,7 +63,7 @@
     return total
 
 
-def body(
+def general_body(
     groups,
     plan_owner,
     plan_slot,
@@ -123,6 +130,353 @@
     return (residual + mixed + bias_two[None, :, None, None]).astype(jnp.bfloat16)
 
 
+def column(row, size):
+    down = lax.broadcasted_iota(jnp.int32, (size, size), 0)
+    across = lax.broadcasted_iota(jnp.int32, (size, size), 1)
+    spread = jnp.where(down == across, jnp.broadcast_to(row, (size, size)), jnp.zeros((), row.dtype))
+    return jnp.sum(spread, axis=1, keepdims=True)
+
+
+def plan_start(owner_ref, slot_ref, states, final, count, per_dev):
+    total = count * per_dev
+    shape = (total, 128)
+    group = lax.broadcasted_iota(jnp.int32, shape, 0)
+    lane = lax.broadcasted_iota(jnp.int32, shape, 1) & (count - 1)
+    owner = jnp.broadcast_to(column(owner_ref[...], total), shape)
+    place = jnp.broadcast_to(column(slot_ref[...], total), shape)
+    source = group // per_dev
+    entry = group - source * per_dev
+    ahead = (owner - source) & (count - 1)
+    forward = ahead < count // 2
+    here = lane == source
+    code = (group << 10) | (place << 8) | entry
+    states[0] = jnp.where(here & forward, ((ahead + 1) << 16) | code, 0)
+    states[1] = jnp.where(here & jnp.logical_not(forward), ((count - ahead) << 16) | code, 0)
+    for s in range(per_dev):
+        for row, at in ((s, count - 1), (per_dev + s, 0)):
+            found = jnp.where(here & (ahead == at) & (place == s), entry, 0)
+            final[pl.ds(row, 1), :] = jnp.max(found, axis=0, keepdims=True)
+
+
+def plan_step(t, states, final, sched, per_dev):
+    group = lax.broadcasted_iota(jnp.int32, states.shape[1:], 0)
+    for way in range(2):
+        state = states[way]
+        arrivals = []
+        for c in range(LANES):
+            best = jnp.max(state, axis=0, keepdims=True)
+            sched[t, pl.ds(way * LANES + c, 1), :] = best & 255
+            state = jnp.where(state == best, 0, state)
+            entry = per_dev + (2 * t + way) * LANES + c
+            moved = jnp.where(best > 0, best - (best & 255) - (1 << 16) + entry, -1)
+            moved = pltpu.roll(moved, 1 if way == 0 else 127, 1)
+            left, slot = moved >> 16, (moved >> 8) & 3
+            for s in range(per_dev):
+                for row, hops in ((s, way), (per_dev + s, 1 - way)):
+                    old = final[pl.ds(row, 1), :]
+                    final[pl.ds(row, 1), :] = jnp.where((left == hops) & (slot == s), entry, old)
+            arrivals.append((moved, left))
+        for moved, left in arrivals:
+            state = jnp.where((group == ((moved >> 10) & 63)) & (left > 0), moved, state)
+        states[way] = state
+
+
+def silu_norm(values, gain):
+    square = jnp.mean(values * values, axis=0, keepdims=True)
+    scaled = values * lax.rsqrt(square + 1e-06) * gain
+    return scaled / (1.0 + jnp.exp(-scaled))
+
+
+def conv_rows(field, weights, mask, at, rows):
+    ch, cols = field.shape[2], field.shape[3]
+    right_side = jnp.concatenate(
+        [field[at : at + 3, r : r + 3].reshape(9 * ch, cols) for r in range(rows)], axis=1
+    )
+    sums = jnp.dot(weights * mask, right_side, preferred_element_type=jnp.float32)
+    lane = lax.broadcasted_iota(jnp.int32, (ch, cols), 1)
+    out = []
+    for r in range(rows):
+        part = sums[:, r * cols : (r + 1) * cols]
+        low = jnp.where(lane == 0, 0.0, pltpu.roll(part[:ch], 1, 1))
+        high = jnp.where(lane == cols - 1, 0.0, pltpu.roll(part[2 * ch :], cols - 1, 1))
+        out.append(part[ch : 2 * ch] + low + high)
+    return out
+
+
+def block_kernel(
+    groups, owner, slot, clips, gain_one, weight_one, bias_one, gain_two, weight_two, bias_two,
+    out, late_out,
+    pool, sending, arrived, beside, states, final, sched, sched_s, final_s, h_one, h_two, timeline, before, stage,
+    late_all, send_sem, recv_sem, side_send, side_recv, sched_sem, span_send, span_recv, late_send, late_recv,
+):
+    spans, places, bands = lax.axis_size("dp"), lax.axis_size("tm"), lax.axis_size("space")
+    dp, tm, sp = lax.axis_index("dp"), lax.axis_index("tm"), lax.axis_index("space")
+    per_dev, rows, ch, cols = out.shape
+    part_rows = rows * ch // PARTS
+    tm_up, tm_down = lax.rem(tm + 1, places), lax.rem(tm + places - 1, places)
+    sp_up, sp_down = lax.rem(sp + 1, bands), lax.rem(sp + bands - 1, bands)
+
+    barrier = pltpu.get_barrier_semaphore()
+    friends = [(dp, tm_up, sp), (dp, tm_down, sp), (dp, tm, sp_up), (dp, tm, sp_down)]
+    friends += [(lax.rem(dp + k, spans), tm, sp) for k in range(1, spans)]
+    for friend in friends:
+        pl.semaphore_signal(barrier, inc=1, device_id=friend, device_id_type=MESH)
+
+    def to_scalars(t):
+        return pltpu.make_async_copy(sched.at[t], sched_s.at[t], sched_sem.at[0])
+
+    def hop(t, way, c, p):
+        k = (2 * t + way) * LANES + c
+        return pltpu.make_async_remote_copy(
+            src_ref=sending.at[k, p], dst_ref=arrived.at[k, p],
+            send_sem=send_sem.at[k, p], recv_sem=recv_sem.at[k, p],
+            device_id=(dp, tm_up if way == 0 else tm_down, sp), device_id_type=MESH,
+        )
+
+    def side(source, entry, p):
+        return pltpu.make_async_remote_copy(
+            src_ref=source, dst_ref=beside.at[entry, 1 - p],
+            send_sem=side_send.at[entry, p], recv_sem=side_recv.at[entry, 1 - p],
+            device_id=(dp, tm, sp_down if p == 0 else sp_up), device_id_type=MESH,
+        )
+
+    def send(t, c, p):
+        for way in range(2):
+            k = (2 * t + way) * LANES + c
+            sending[k, p] = pool[sched_s[t, way * LANES + c, tm], p]
+            hop(t, way, c, p).start()
+
+    def receive(t, c, p):
+        for way in range(2):
+            k = (2 * t + way) * LANES + c
+            hop(t, way, c, p).wait()
+            pool[per_dev + k, p] = arrived[k, p]
+
+    def share(t, c, p):
+        for way in range(2):
+            k = (2 * t + way) * LANES + c
+            side(arrived.at[k, p], per_dev + k, p).start()
+
+    plan_start(owner, slot, states, final, places, per_dev)
+    plan_step(0, states, final, sched, per_dev)
+    to_scalars(0).start()
+    for f in range(per_dev):
+        for p in range(PARTS):
+            pool[f, p] = groups[f, p * part_rows : (p + 1) * part_rows]
+    to_scalars(0).wait()
+    pl.semaphore_wait(barrier, len(friends))
+
+    for c in range(LANES):
+        for p in range(PARTS):
+            send(0, c, p)
+    for f in range(per_dev):
+        for p in range(PARTS):
+            side(groups.at[f, pl.ds(p * part_rows, part_rows)], f, p).start()
+    plan_step(1, states, final, sched, per_dev)
+    to_scalars(1).start()
+
+    def turn(t):
+        to_scalars(t).wait()
+        for c in range(LANES):
+            for p in range(PARTS):
+                receive(t - 1, c, p)
+                send(t, c, p)
+                share(t - 1, c, p)
+
+    def step(t, carry):
+        turn(t)
+        plan_step(t + 1, states, final, sched, per_dev)
+        to_scalars(t + 1).start()
+        return carry
+
+    lax.fori_loop(1, STEPS - 1, step, 0)
+    turn(STEPS - 1)
+
+    final_copy = pltpu.make_async_copy(final, final_s, sched_sem.at[1])
+    final_copy.start()
+    late = jnp.max(jnp.maximum(states[0], states[1]), axis=0, keepdims=True)
+    late = jnp.max(late, axis=1, keepdims=True)
+    late_all[0] = jnp.broadcast_to((late > 0).astype(jnp.float32), (8, 128))
+    late_copies = []
+    for k in range(1, spans):
+        copy = pltpu.make_async_remote_copy(
+            src_ref=late_all.at[0], dst_ref=late_all.at[k], send_sem=late_send.at[k - 1],
+            recv_sem=late_recv.at[k - 1], device_id=(lax.rem(dp + k, spans), tm, sp), device_id_type=MESH,
+        )
+        copy.start()
+        late_copies.append(copy)
+    gain_a = column(gain_one[...], ch)
+    gain_b = column(gain_two[...], ch)
+    bias_a = column(bias_one[...], ch)
+    bias_b = column(bias_two[...], ch)
+    first = (dp * places + tm) * per_dev
+    tap = lax.broadcasted_iota(jnp.int32, (1, 9 * ch), 1) // (3 * ch)
+    masks = []
+    for s in range(-2, per_dev):
+        start, latest = jnp.int32(0), jnp.int32(0)
+        for c in range(clips.shape[1]):
+            latest = jnp.where(start <= first + s, start, latest)
+            start = start + clips[0, c]
+        masks.append((2 - tap <= first + s - latest).astype(jnp.float32).astype(jnp.bfloat16))
+    final_copy.wait()
+    entries = [final_s[f, tm] for f in range(2 * per_dev)]
+
+    for c in range(LANES):
+        for p in range(PARTS):
+            receive(STEPS - 1, c, p)
+            share(STEPS - 1, c, p)
+
+    def to_next(k):
+        return pltpu.make_async_remote_copy(
+            src_ref=stage.at[k], dst_ref=before.at[k], send_sem=span_send.at[k], recv_sem=span_recv.at[k],
+            device_id=(lax.rem(dp + 1, spans), tm, sp), device_id_type=MESH,
+        )
+
+    def norm_rows(f, at, values):
+        for r in range(2):
+            h_one[f, at + r] = silu_norm(
+                values[r * ch : (r + 1) * ch].astype(jnp.float32), gain_a
+            ).astype(jnp.bfloat16)
+
+    def outside(field, low, high):
+        @pl.when(sp == 0)
+        def _():
+            field[:, :low] = jnp.zeros((field.shape[0], low, ch, cols), field.dtype)
+
+        @pl.when(sp == bands - 1)
+        def _():
+            field[:, high:] = jnp.zeros((field.shape[0], field.shape[1] - high, ch, cols), field.dtype)
+
+    @pl.when(tm == 0)
+    def _():
+        for f in range(per_dev):
+            for p in range(PARTS):
+                stage[0, f, p] = pool[entries[f], p]
+        to_next(0).start()
+
+    for f in range(2 * per_dev):
+        for p in range(PARTS):
+            values = pool[entries[f], p]
+            if f >= per_dev:
+                timeline[f - per_dev, p] = values
+            norm_rows(f, 2 + 2 * p, values)
+
+    def side_wait(entry, carry):
+        for p in range(PARTS):
+            side(arrived.at[0, p], entry, p).wait_send()
+            side(arrived.at[0, p], entry, 1 - p).wait_recv()
+        return carry
+
+    lax.fori_loop(0, per_dev + 2 * LANES * STEPS, side_wait, 0)
+
+    @pl.when(tm == 0)
+    def _():
+        for f in range(per_dev):
+            for p in range(2):
+                stage[1, f, p] = beside[entries[f], p]
+        to_next(1).start()
+
+    for f in range(2 * per_dev):
+        for p in range(2):
+            norm_rows(f, 6 * p, beside[entries[f], p])
+    outside(h_one, 2, rows + 2)
+
+    def first_conv(j):
+        for r, act in enumerate(conv_rows(h_one, weight_one[...], masks[j], j, rows + 2)):
+            h_two[j, r] = silu_norm(act + bias_a, gain_b).astype(jnp.bfloat16)
+
+    first_conv(5)
+    first_conv(4)
+
+    @pl.when(tm == 0)
+    def _():
+        for k in range(2):
+            to_next(k).wait()
+        for f in range(per_dev):
+            for p in range(PARTS):
+                norm_rows(f, 2 + 2 * p, before[0, f, p])
+                norm_rows(f, 6 * p, before[1, f, p])
+        outside(h_one, 2, rows + 2)
+
+    for j in (3, 2, 1, 0):
+        first_conv(j)
+    outside(h_two, 1, rows + 1)
+    for s in (3, 2, 1, 0):
+        for r, mixed in enumerate(conv_rows(h_two, weight_two[...], masks[s + 2], s, rows)):
+            p, at = divmod(r * ch, part_rows)
+            kept = timeline[s, p, at : at + ch].astype(jnp.float32)
+            out[s, r] = (kept + mixed + bias_b).astype(jnp.bfloat16)
+
+    for copy in late_copies:
+        copy.wait()
+    late_out[...] = jnp.max(late_all[...], axis=0)
+
+
+def fast_body(
+    groups, plan_owner, plan_slot, clip_lengths, gain_one, weight_one, bias_one, gain_two, weight_two, bias_two
+):
+    per_dev, _, ch, rows, cols = groups.shape
+    spans = lax.axis_size("dp")
+    turned = jnp.transpose(groups[:, 0], (0, 2, 1, 3)).reshape(per_dev, rows * ch, cols)
+    weights = [
+        jnp.transpose(w, (2, 3, 0, 1, 4)).reshape(3 * ch, 9 * ch) for w in (weight_one, weight_two)
+    ]
+    vmem, smem = pl.BlockSpec(memory_space=pltpu.VMEM), pl.BlockSpec(memory_space=pltpu.SMEM)
+    part = (PARTS, rows * ch // PARTS, cols)
+    sends = 2 * LANES * STEPS
+    return pl.pallas_call(
+        block_kernel,
+        out_shape=(
+            jax.ShapeDtypeStruct((per_dev, rows, ch, cols), jnp.bfloat16),
+            jax.ShapeDtypeStruct((8, 128), jnp.float32),
+        ),
+        in_specs=[vmem, vmem, vmem, smem] + [vmem] * 6,
+        out_specs=(vmem, vmem),
+        scratch_shapes=[
+            pltpu.VMEM((per_dev + sends,) + part, jnp.bfloat16),
+            pltpu.VMEM((sends,) + part, jnp.bfloat16),
+            pltpu.VMEM((sends,) + part, jnp.bfloat16),
+            pltpu.VMEM((per_dev + sends,) + part, jnp.bfloat16),
+            pltpu.VMEM((2, plan_owner.shape[1], 128), jnp.int32),
+            pltpu.VMEM((8, 128), jnp.int32),
+            pltpu.VMEM((STEPS, 8, 128), jnp.int32),
+            pltpu.SMEM((STEPS, 8, 128), jnp.int32),
+            pltpu.SMEM((8, 128), jnp.int32),
+            pltpu.VMEM((2 * per_dev, rows + 4, ch, cols), jnp.bfloat16),
+            pltpu.VMEM((per_dev + 2, rows + 2, ch, cols), jnp.bfloat16),
+            pltpu.VMEM((per_dev,) + part, jnp.bfloat16),
+            pltpu.VMEM((2, per_dev) + part, jnp.bfloat16),
+            pltpu.VMEM((2, per_dev) + part, jnp.bfloat16),
+            pltpu.VMEM((spans, 8, 128), jnp.float32),
+            pltpu.SemaphoreType.DMA((sends, PARTS)),
+            pltpu.SemaphoreType.DMA((sends, PARTS)),
+            pltpu.SemaphoreType.DMA((per_dev + sends, PARTS)),
+            pltpu.SemaphoreType.DMA((per_dev + sends, PARTS)),
+            pltpu.SemaphoreType.DMA((2,)),
+            pltpu.SemaphoreType.DMA((2,)),
+            pltpu.SemaphoreType.DMA((2,)),
+            pltpu.SemaphoreType.DMA((spans - 1,)),
+            pltpu.SemaphoreType.DMA((spans - 1,)),
+        ],
+        compiler_params=pltpu.CompilerParams(
+            collective_id=0, has_side_effects=True, vmem_limit_bytes=48 * 2**20
+        ),
+    )(
+        turned, plan_owner, plan_slot, clip_lengths[None], gain_one[None], weights[0], bias_one[None],
+        gain_two[None], weights[1], bias_two[None],
+    )
+
+
+def body(*args):
+    fast, late = fast_body(*args)
+    return lax.cond(
+        late[0, 0] > 0,
+        lambda *args: general_body(*args),
+        lambda *args: jnp.transpose(fast, (0, 2, 1, 3)),
+        *args,
+    )
+
+
 def solution(mesh):
     return jax.shard_map(
         body,

time: 159 us -> 73.2 us (0.46)
  the two profiles are of different devices: /device:TPU:6 before, /device:TPU:1 now
where the time goes in v2:
time: 73.2 us; the launch traced here: 73.1 us
  Pallas kernels  67.1 us (92%)
  local copies, waits for them, and re-layouts  4.85 us (7%)
  between operations  0.86 us (1%)
    pallas_call x1, Pallas kernels, fast_body(): pl.pallas_call(block_kernel, out_shape=(jax.ShapeDtypeStruct((per_dev, ro...  67.1 us
    transpose x2, local copies, waits for them, and re-layouts, fast_body(): jnp.transpose(w, (2, 3, 0, 1, 4)).reshape(3 * ch, 9 * ch)  2.07 us

profile of v2, /device:TPU:1, one launch (start us, length us, event | category | flops | bytes accessed | tf_op | source)
XLA Modules:
  0.0 73.1 jit_solution(11984576777729017477)
XLA Ops:
  0.0 1.6 %copy.134 = bf16[3,96,3,3,96]{4,3,2,1,0:T(4,128)(2,1)S(1)} copy(bf16[3,96,3,3,96]{4,1,0,3,2:T(8,128)(2,1)} %bitcast.254) | data formatting | bytes 995328 | tf_op jit(solution)/shard_map/transpose | solution.py:422
  1.6 0.6 reshape.240.weight_one
  2.2 0.0 copy-start.4
  2.2 0.0 copy-done.2
  2.2 0.0 copy-start.6
  2.3 0.0 copy-start.7
  2.3 0.0 copy-start.8
  2.3 0.0 copy-start.9
  2.3 0.0 copy-start.10
  2.3 0.0 copy-start.11
  2.3 0.0 copy-start.12
  2.3 0.5 copy.135
  2.8 0.0 copy-start.1
  2.8 0.6 reshape.241.weight_two
  3.4 0.0 copy-done.4
  3.4 0.1 copy.133
  3.5 0.0 copy-done.6
  3.5 0.0 copy-done.7
  3.6 67.1 %shard_map.102 = (bf16[4,4,96,128]{3,2,1,0:T(8,128)(2,1)S(1)}, f32[8,128]{1,0:T(8,128)S(1)}) custom-call(bf16[4,384,128]{2,1,0:T(8,128)(2,1)S(1)} %bitcast.217, s32[1,64]{1,0:T(1,128)S(1)} %copy-done.10, s32[1,64]{1,0:T(1,128)S(1)} %copy-done.11, s32[1,12]{1,0:T(1,128)S(1)} %bitcast.262, f32[1,96]{1,0:T(1,128)S(1)} %bitcast.258, ...), custom_call_target="tpu_custom_call" | custom-call | tf_op jit(solution)/shard_map/pallas_call | solution.py:427
  70.7 0.5 slice.164
  71.9 0.4 conditional.1
  71.9 0.2 copy.157
  72.3 0.0 copy-start.5
  72.3 0.7 %copy-done.5 = bf16[4,96,4,128]{3,2,1,0:T(4,128)(2,1)} copy-done((bf16[4,96,4,128]{3,2,1,0:T(4,128)(2,1)}, bf16[4,96,4,128]{3,2,1,0:T(4,128)(2,1)S(1)}, u32[]{:S(2)}) %copy-start.5) | copy-done | bytes 393240
  (7 shorter events, 0.0 us)
Async XLA Ops:
  0.0 2.2 %copy-start.2 = (bf16[3,3,3,96,96]{4,3,2,1,0:T(8,128)(2,1)S(1)}, bf16[3,3,3,96,96]{4,3,2,1,0:T(8,128)(2,1)}, u32[]{:S(2)}) copy-start(bf16[3,3,3,96,96]{4,3,2,1,0:T(8,128)(2,1)} %param.20) | copy-start | bytes 1492996
  2.2 1.2 %copy-start.4 = (bf16[4,1,96,4,128]{4,3,2,1,0:T(4,128)(2,1)S(1)}, bf16[4,1,96,4,128]{4,3,2,1,0:T(4,128)(2,1)}, u32[]{:S(2)}) copy-start(bf16[4,1,96,4,128]{4,3,2,1,0:T(4,128)(2,1)} %param.12) | copy-start | bytes 1179652
  2.2 1.2 %copy-start.6 = (f32[96]{0:T(128)S(1)}, f32[96]{0:T(128)}, u32[]{:S(2)}) copy-start(f32[96]{0:T(128)} %param.16) | copy-start | bytes 1156
  2.3 1.2 %copy-start.7 = (f32[96]{0:T(128)S(1)}, f32[96]{0:T(128)}, u32[]{:S(2)}) copy-start(f32[96]{0:T(128)} %param.18) | copy-start | bytes 1156
  2.3 1.2 %copy-start.8 = (f32[96]{0:T(128)S(1)}, f32[96]{0:T(128)}, u32[]{:S(2)}) copy-start(f32[96]{0:T(128)} %param.19) | copy-start | bytes 1156
  2.3 1.2 %copy-start.9 = (f32[96]{0:T(128)S(1)}, f32[96]{0:T(128)}, u32[]{:S(2)}) copy-start(f32[96]{0:T(128)} %param.21) | copy-start | bytes 1156
  2.3 1.2 %copy-start.10 = (s32[1,64]{1,0:T(1,128)S(1)}, s32[1,64]{1,0:T(1,128)}, u32[]{:S(2)}) copy-start(s32[1,64]{1,0:T(1,128)} %owner.1) | copy-start | bytes 772
  2.3 1.2 %copy-start.11 = (s32[1,64]{1,0:T(1,128)S(1)}, s32[1,64]{1,0:T(1,128)}, u32[]{:S(2)}) copy-start(s32[1,64]{1,0:T(1,128)} %slot.1) | copy-start | bytes 772
  2.3 1.2 %copy-start.12 = (s32[12]{0:T(128)S(1)}, s32[12]{0:T(128)}, u32[]{:S(2)}) copy-start(s32[12]{0:T(128)} %param.15) | copy-start | bytes 148
  2.8 69.1 %copy-start.1 = (bf16[3,3,3,96,96]{4,3,2,1,0:T(8,128)(2,1)S(1)}, bf16[3,3,3,96,96]{4,3,2,1,0:T(8,128)(2,1)}, u32[]{:S(2)}) copy-start(bf16[3,3,3,96,96]{4,3,2,1,0:T(8,128)(2,1)} %param.17) | copy-start | bytes 1492996
  72.3 0.7 %copy-start.5 = (bf16[4,96,4,128]{3,2,1,0:T(4,128)(2,1)}, bf16[4,96,4,128]{3,2,1,0:T(4,128)(2,1)S(1)}, u32[]{:S(2)}) copy-start(bf16[4,96,4,128]{3,2,1,0:T(4,128)(2,1)S(1)} %get-tuple-element.105) | copy-start | bytes 1179652

commit v3 on v2

--- a/solution.py
+++ b/solution.py
@@ -206,12 +206,14 @@
 def block_kernel(
     groups, owner, slot, clips, gain_one, weight_one, bias_one, gain_two, weight_two, bias_two,
     out, late_out,
-    pool, sending, arrived, beside, states, final, sched, sched_s, final_s, h_one, h_two, timeline, before, stage,
-    late_all, send_sem, recv_sem, side_send, side_recv, sched_sem, span_send, span_recv, late_send, late_recv,
+    pool, sending, arrived, beside, beside_last, states, final, sched, sched_s, final_s, h_one, h_two, timeline, before, stage,
+    late_all, before_final, before_final_s, raw, stacked, back,
+    send_sem, recv_sem, side_send, side_recv, sched_sem, span_send, span_recv, late_send, late_recv, raw_sem,
 ):
     spans, places, bands = lax.axis_size("dp"), lax.axis_size("tm"), lax.axis_size("space")
     dp, tm, sp = lax.axis_index("dp"), lax.axis_index("tm"), lax.axis_index("space")
-    per_dev, rows, ch, cols = out.shape
+    per_dev, cols, ch = out.shape[0], out.shape[2], h_one.shape[2]
+    rows = out.shape[1] // ch
     part_rows = rows * ch // PARTS
     tm_up, tm_down = lax.rem(tm + 1, places), lax.rem(tm + places - 1, places)
     sp_up, sp_down = lax.rem(sp + 1, bands), lax.rem(sp + bands - 1, bands)
@@ -219,50 +221,74 @@
     barrier = pltpu.get_barrier_semaphore()
     friends = [(dp, tm_up, sp), (dp, tm_down, sp), (dp, tm, sp_up), (dp, tm, sp_down)]
     friends += [(lax.rem(dp + k, spans), tm, sp) for k in range(1, spans)]
+    dp_next = jnp.where(tm == places - 1, lax.rem(dp + 1, spans), dp)
+    dp_prev = jnp.where(tm == 0, lax.rem(dp + spans - 1, spans), dp)
+    friends += [(dp_next, tm_up, sp), (dp_prev, tm_down, sp)]
     for friend in friends:
         pl.semaphore_signal(barrier, inc=1, device_id=friend, device_id_type=MESH)
 
     def to_scalars(t):
         return pltpu.make_async_copy(sched.at[t], sched_s.at[t], sched_sem.at[0])
 
-    def hop(t, way, c, p):
-        k = (2 * t + way) * LANES + c
+    last = per_dev + 2 * LANES * (STEPS - 1)
+
+    def hop(t, c, p, way):
+        ends = isinstance(t, int) and t == STEPS - 1 and way == 0
+        at = (t * LANES + c, p) if way is None else (t * LANES + c, p, way)
         return pltpu.make_async_remote_copy(
-            src_ref=sending.at[k, p], dst_ref=arrived.at[k, p],
-            send_sem=send_sem.at[k, p], recv_sem=recv_sem.at[k, p],
-            device_id=(dp, tm_up if way == 0 else tm_down, sp), device_id_type=MESH,
+            src_ref=sending.at[at], dst_ref=arrived.at[at],
+            send_sem=send_sem.at[lax.rem(t, 2), c, p], recv_sem=recv_sem.at[t, c, p],
+            device_id=(dp_next if ends else dp, tm_down if way == 1 else tm_up, sp), device_id_type=MESH,
         )
 
     def side(source, entry, p):
+        block = entry // (2 * LANES)
+        here = beside_last.at[entry - last] if isinstance(entry, int) and entry >= last else beside.at[entry]
         return pltpu.make_async_remote_copy(
-            src_ref=source, dst_ref=beside.at[entry, 1 - p],
-            send_sem=side_send.at[entry, p], recv_sem=side_recv.at[entry, 1 - p],
+            src_ref=source, dst_ref=here.at[1 - p], send_sem=side_send.at[block], recv_sem=side_recv.at[block],
             device_id=(dp, tm, sp_down if p == 0 else sp_up), device_id_type=MESH,
         )
 
+    def side_wait(block):
+        every = beside.at[pl.ds(0, 2 * LANES)]
+        pltpu.make_async_remote_copy(
+            src_ref=every, dst_ref=beside_last if isinstance(block, int) and block == STEPS else beside.at[
+                pl.ds(2 * LANES * block, 2 * LANES)
+            ],
+            send_sem=side_send.at[block], recv_sem=side_recv.at[block],
+            device_id=(dp, tm, sp_up), device_id_type=MESH,
+        ).wait()
+
     def send(t, c, p):
         for way in range(2):
-            k = (2 * t + way) * LANES + c
-            sending[k, p] = pool[sched_s[t, way * LANES + c, tm], p]
-            hop(t, way, c, p).start()
+            sending[t * LANES + c, p, way] = pool[sched_s[t, way * LANES + c, tm], p]
+            hop(t, c, p, way).start()
 
     def receive(t, c, p):
+        hop(t, c, p, None).wait()
         for way in range(2):
-            k = (2 * t + way) * LANES + c
-            hop(t, way, c, p).wait()
-            pool[per_dev + k, p] = arrived[k, p]
+            pool[per_dev + (2 * t + way) * LANES + c, p] = arrived[t * LANES + c, p, way]
 
     def share(t, c, p):
         for way in range(2):
-            k = (2 * t + way) * LANES + c
-            side(arrived.at[k, p], per_dev + k, p).start()
-
+            side(arrived.at[t * LANES + c, p, way], per_dev + (2 * t + way) * LANES + c, p).start()
+
+    raws = [pltpu.make_async_copy(w, raw.at[k], raw_sem.at[k]) for k, w in enumerate((weight_one, weight_two))]
+    for copy in raws:
+        copy.start()
     plan_start(owner, slot, states, final, places, per_dev)
     plan_step(0, states, final, sched, per_dev)
     to_scalars(0).start()
+    size = rows * ch
+    down = lax.broadcasted_iota(jnp.int32, (size, size), 0)
+    across = lax.broadcasted_iota(jnp.int32, (size, size), 1)
+    turn_rows = ((across & (rows - 1)) * ch + across // rows == down).astype(jnp.float32).astype(jnp.bfloat16)
+    mine = jnp.dot(
+        turn_rows, jnp.concatenate([groups[f] for f in range(per_dev)], axis=1), preferred_element_type=jnp.float32
+    ).astype(jnp.bfloat16)
     for f in range(per_dev):
         for p in range(PARTS):
-            pool[f, p] = groups[f, p * part_rows : (p + 1) * part_rows]
+            pool[f, p] = mine[p * part_rows : (p + 1) * part_rows, f * cols : (f + 1) * cols]
     to_scalars(0).wait()
     pl.semaphore_wait(barrier, len(friends))
 
@@ -271,9 +297,13 @@
             send(0, c, p)
     for f in range(per_dev):
         for p in range(PARTS):
-            side(groups.at[f, pl.ds(p * part_rows, part_rows)], f, p).start()
+            side(pool.at[f, p], f, p).start()
     plan_step(1, states, final, sched, per_dev)
     to_scalars(1).start()
+    for k, copy in enumerate(raws):
+        copy.wait()
+        stacked[k] = jnp.concatenate([raw[k, j] for j in range(9)], axis=1)
+    back[...] = ((down & (rows - 1)) * ch + down // rows == across).astype(jnp.float32).astype(jnp.bfloat16)
 
     def turn(t):
         to_scalars(t).wait()
@@ -282,6 +312,7 @@
                 receive(t - 1, c, p)
                 send(t, c, p)
                 share(t - 1, c, p)
+        side_wait(t - 1)
 
     def step(t, carry):
         turn(t)
@@ -290,21 +321,43 @@
         return carry
 
     lax.fori_loop(1, STEPS - 1, step, 0)
-    turn(STEPS - 1)
-
     final_copy = pltpu.make_async_copy(final, final_s, sched_sem.at[1])
     final_copy.start()
+    turn(STEPS - 1)
+
+    final_copy.wait()
+    entries = [final_s[f, tm] for f in range(2 * per_dev)]
+
+    span_copies = []
+    for j, part in enumerate((pl.ds(1, PARTS), 0, 3)):
+        span_copies.append(pltpu.make_async_remote_copy(
+            src_ref=stage.at[:, part], dst_ref=before.at[pl.ds(0, per_dev), part],
+            send_sem=span_send.at[j], recv_sem=span_recv.at[j],
+            device_id=(lax.rem(dp + 1, spans), tm, sp), device_id_type=MESH,
+        ))
+    final_next = pltpu.make_async_remote_copy(
+        src_ref=final, dst_ref=before_final, send_sem=span_send.at[3], recv_sem=span_recv.at[3],
+        device_id=(lax.rem(dp + 1, spans), tm, sp), device_id_type=MESH,
+    )
+
+    @pl.when(tm == 0)
+    def _():
+        for f in range(per_dev):
+            entry = jnp.where(entries[f] >= last, 0, entries[f])
+            for p in range(PARTS):
+                stage[f, 1 + p] = pool[entry, p]
+        span_copies[0].start()
+        final_next.start()
+
     late = jnp.max(jnp.maximum(states[0], states[1]), axis=0, keepdims=True)
     late = jnp.max(late, axis=1, keepdims=True)
     late_all[0] = jnp.broadcast_to((late > 0).astype(jnp.float32), (8, 128))
-    late_copies = []
     for k in range(1, spans):
         copy = pltpu.make_async_remote_copy(
-            src_ref=late_all.at[0], dst_ref=late_all.at[k], send_sem=late_send.at[k - 1],
-            recv_sem=late_recv.at[k - 1], device_id=(lax.rem(dp + k, spans), tm, sp), device_id_type=MESH,
+            src_ref=late_all.at[0], dst_ref=late_all.at[k], send_sem=late_send, recv_sem=late_recv,
+            device_id=(lax.rem(dp + k, spans), tm, sp), device_id_type=MESH,
         )
         copy.start()
-        late_copies.append(copy)
     gain_a = column(gain_one[...], ch)
     gain_b = column(gain_two[...], ch)
     bias_a = column(bias_one[...], ch)
@@ -318,19 +371,21 @@
             latest = jnp.where(start <= first + s, start, latest)
             start = start + clips[0, c]
         masks.append((2 - tap <= first + s - latest).astype(jnp.float32).astype(jnp.bfloat16))
-    final_copy.wait()
-    entries = [final_s[f, tm] for f in range(2 * per_dev)]
-
     for c in range(LANES):
         for p in range(PARTS):
             receive(STEPS - 1, c, p)
             share(STEPS - 1, c, p)
-
-    def to_next(k):
-        return pltpu.make_async_remote_copy(
-            src_ref=stage.at[k], dst_ref=before.at[k], send_sem=span_send.at[k], recv_sem=span_recv.at[k],
-            device_id=(lax.rem(dp + 1, spans), tm, sp), device_id_type=MESH,
-        )
+        if c == 0:
+            side_wait(STEPS - 1)
+
+            @pl.when(tm == 0)
+            def _():
+                for f in range(per_dev):
+                    entry = jnp.where(entries[f] >= last, 0, entries[f])
+                    for p in range(2):
+                        stage[f, 3 * p] = beside[entry, p]
+                for copy in span_copies[1:]:
+                    copy.start()
 
     def norm_rows(f, at, values):
         for r in range(2):
@@ -346,13 +401,6 @@
         @pl.when(sp == bands - 1)
         def _():
             field[:, high:] = jnp.zeros((field.shape[0], field.shape[1] - high, ch, cols), field.dtype)
-
-    @pl.when(tm == 0)
-    def _():
-        for f in range(per_dev):
-            for p in range(PARTS):
-                stage[0, f, p] = pool[entries[f], p]
-        to_next(0).start()
 
     for f in range(2 * per_dev):
         for p in range(PARTS):
@@ -361,28 +409,18 @@
                 timeline[f - per_dev, p] = values
             norm_rows(f, 2 + 2 * p, values)
 
-    def side_wait(entry, carry):
-        for p in range(PARTS):
-            side(arrived.at[0, p], entry, p).wait_send()
-            side(arrived.at[0, p], entry, 1 - p).wait_recv()
-        return carry
-
-    lax.fori_loop(0, per_dev + 2 * LANES * STEPS, side_wait, 0)
-
-    @pl.when(tm == 0)
-    def _():
-        for f in range(per_dev):
-            for p in range(2):
-                stage[1, f, p] = beside[entries[f], p]
-        to_next(1).start()
-
+    side_wait(STEPS)
+
+    for k in range(2 * LANES):
+        for p in range(2):
+            beside[last + k, p] = beside_last[k, p]
     for f in range(2 * per_dev):
         for p in range(2):
             norm_rows(f, 6 * p, beside[entries[f], p])
     outside(h_one, 2, rows + 2)
 
     def first_conv(j):
-        for r, act in enumerate(conv_rows(h_one, weight_one[...], masks[j], j, rows + 2)):
+        for r, act in enumerate(conv_rows(h_one, stacked[0], masks[j], j, rows + 2)):
             h_two[j, r] = silu_norm(act + bias_a, gain_b).astype(jnp.bfloat16)
 
     first_conv(5)
@@ -390,25 +428,42 @@
 
     @pl.when(tm == 0)
     def _():
-        for k in range(2):
-            to_next(k).wait()
+        final_next.wait()
+        move = pltpu.make_async_copy(before_final, before_final_s, sched_sem.at[1])
+        move.start()
+        for c in range(LANES):
+            for p in range(2):
+                before[per_dev + c, 1 + p] = pool[last + c, p]
+                before[per_dev + c, 3 * p] = beside_last[c, p]
+        for copy in span_copies:
+            copy.wait()
+        move.wait()
         for f in range(per_dev):
-            for p in range(PARTS):
-                norm_rows(f, 2 + 2 * p, before[0, f, p])
-                norm_rows(f, 6 * p, before[1, f, p])
+            entry = before_final_s[f, 0]
+            entry = jnp.where(entry >= last, per_dev + jnp.minimum(entry - last, LANES - 1), f)
+            for q in range(4):
+                norm_rows(f, 2 * q, before[entry, q])
         outside(h_one, 2, rows + 2)
 
     for j in (3, 2, 1, 0):
         first_conv(j)
     outside(h_two, 1, rows + 1)
-    for s in (3, 2, 1, 0):
-        for r, mixed in enumerate(conv_rows(h_two, weight_two[...], masks[s + 2], s, rows)):
-            p, at = divmod(r * ch, part_rows)
-            kept = timeline[s, p, at : at + ch].astype(jnp.float32)
-            out[s, r] = (kept + mixed + bias_b).astype(jnp.bfloat16)
-
-    for copy in late_copies:
-        copy.wait()
+    for pair in ((3, 2), (1, 0)):
+        ready = []
+        for s in pair:
+            mixed = jnp.concatenate(conv_rows(h_two, stacked[1], masks[s + 2], s, rows), axis=0)
+            kept = timeline[s].reshape(size, cols).astype(jnp.float32)
+            bias = jnp.concatenate([bias_b] * rows, axis=0)
+            ready.append((kept + mixed + bias).astype(jnp.bfloat16))
+        turned = jnp.dot(back[...], jnp.concatenate(ready, axis=1), preferred_element_type=jnp.float32)
+        for k, s in enumerate(pair):
+            out[s] = turned[:, k * cols : (k + 1) * cols].astype(jnp.bfloat16)
+
+    others = late_all.at[pl.ds(1, spans - 1)]
+    pltpu.make_async_remote_copy(
+        src_ref=others, dst_ref=others, send_sem=late_send, recv_sem=late_recv,
+        device_id=(lax.rem(dp + 1, spans), tm, sp), device_id_type=MESH,
+    ).wait()
     late_out[...] = jnp.max(late_all[...], axis=0)
 
 
@@ -417,26 +472,24 @@
 ):
     per_dev, _, ch, rows, cols = groups.shape
     spans = lax.axis_size("dp")
-    turned = jnp.transpose(groups[:, 0], (0, 2, 1, 3)).reshape(per_dev, rows * ch, cols)
-    weights = [
-        jnp.transpose(w, (2, 3, 0, 1, 4)).reshape(3 * ch, 9 * ch) for w in (weight_one, weight_two)
-    ]
     vmem, smem = pl.BlockSpec(memory_space=pltpu.VMEM), pl.BlockSpec(memory_space=pltpu.SMEM)
+    whole = pl.BlockSpec(memory_space=pl.ANY)
     part = (PARTS, rows * ch // PARTS, cols)
     sends = 2 * LANES * STEPS
     return pl.pallas_call(
         block_kernel,
         out_shape=(
-            jax.ShapeDtypeStruct((per_dev, rows, ch, cols), jnp.bfloat16),
+            jax.ShapeDtypeStruct((per_dev, rows * ch, cols), jnp.bfloat16),
             jax.ShapeDtypeStruct((8, 128), jnp.float32),
         ),
-        in_specs=[vmem, vmem, vmem, smem] + [vmem] * 6,
+        in_specs=[vmem, vmem, vmem, smem, vmem, whole, vmem, vmem, whole, vmem],
         out_specs=(vmem, vmem),
         scratch_shapes=[
             pltpu.VMEM((per_dev + sends,) + part, jnp.bfloat16),
-            pltpu.VMEM((sends,) + part, jnp.bfloat16),
-            pltpu.VMEM((sends,) + part, jnp.bfloat16),
+            pltpu.VMEM((STEPS * LANES, PARTS, 2) + part[1:], jnp.bfloat16),
+            pltpu.VMEM((STEPS * LANES, PARTS, 2) + part[1:], jnp.bfloat16),
             pltpu.VMEM((per_dev + sends,) + part, jnp.bfloat16),
+            pltpu.VMEM((2 * LANES,) + part, jnp.bfloat16),
             pltpu.VMEM((2, plan_owner.shape[1], 128), jnp.int32),
             pltpu.VMEM((8, 128), jnp.int32),
             pltpu.VMEM((STEPS, 8, 128), jnp.int32),
@@ -445,25 +498,32 @@
             pltpu.VMEM((2 * per_dev, rows + 4, ch, cols), jnp.bfloat16),
             pltpu.VMEM((per_dev + 2, rows + 2, ch, cols), jnp.bfloat16),
             pltpu.VMEM((per_dev,) + part, jnp.bfloat16),
-            pltpu.VMEM((2, per_dev) + part, jnp.bfloat16),
-            pltpu.VMEM((2, per_dev) + part, jnp.bfloat16),
+            pltpu.VMEM((per_dev + LANES, 4) + part[1:], jnp.bfloat16),
+            pltpu.VMEM((per_dev, 4) + part[1:], jnp.bfloat16),
             pltpu.VMEM((spans, 8, 128), jnp.float32),
-            pltpu.SemaphoreType.DMA((sends, PARTS)),
-            pltpu.SemaphoreType.DMA((sends, PARTS)),
-            pltpu.SemaphoreType.DMA((per_dev + sends, PARTS)),
-            pltpu.SemaphoreType.DMA((per_dev + sends, PARTS)),
+            pltpu.VMEM((8, 128), jnp.int32),
+            pltpu.SMEM((8, 128), jnp.int32),
+            pltpu.VMEM((2, 9, 3 * ch, ch), jnp.bfloat16),
+            pltpu.VMEM((2, 3 * ch, 9 * ch), jnp.bfloat16),
+            pltpu.VMEM((rows * ch, rows * ch), jnp.bfloat16),
+            pltpu.SemaphoreType.DMA((2, LANES, PARTS)),
+            pltpu.SemaphoreType.DMA((STEPS, LANES, PARTS)),
+            pltpu.SemaphoreType.DMA((STEPS + 1,)),
+            pltpu.SemaphoreType.DMA((STEPS + 1,)),
             pltpu.SemaphoreType.DMA((2,)),
+            pltpu.SemaphoreType.DMA((4,)),
+            pltpu.SemaphoreType.DMA((4,)),
+            pltpu.SemaphoreType.DMA,
+            pltpu.SemaphoreType.DMA,
             pltpu.SemaphoreType.DMA((2,)),
-            pltpu.SemaphoreType.DMA((2,)),
-            pltpu.SemaphoreType.DMA((spans - 1,)),
-            pltpu.SemaphoreType.DMA((spans - 1,)),
         ],
         compiler_params=pltpu.CompilerParams(
             collective_id=0, has_side_effects=True, vmem_limit_bytes=48 * 2**20
         ),
     )(
-        turned, plan_owner, plan_slot, clip_lengths[None], gain_one[None], weights[0], bias_one[None],
-        gain_two[None], weights[1], bias_two[None],
+        groups.reshape(per_dev, ch * rows, cols), plan_owner, plan_slot, clip_lengths[None], gain_one[None],
+        weight_one.reshape(9, 3 * ch, ch), bias_one[None], gain_two[None], weight_two.reshape(9, 3 * ch, ch),
+        bias_two[None],
     )
 
 
@@ -472,7 +532,7 @@
     return lax.cond(
         late[0, 0] > 0,
         lambda *args: general_body(*args),
-        lambda *args: jnp.transpose(fast, (0, 2, 1, 3)),
+        lambda *args: fast.reshape(args[0].shape[:1] + args[0].shape[2:]),
         *args,
     )
 

time: 73.2 us -> 66.7 us (0.911)
  local copies, waits for them, and re-layouts: 4.85 us -> 1.26 us
  Pallas kernels: 67.1 us -> 64.4 us
    pallas_call x1, Pallas kernels: 67.1 us -> 64.4 us  [fast_body(): pl.pallas_call(block_kernel, out_shape=(jax.ShapeDtypeStruct((per_dev, ro...]
    transpose x3 -> x0, local copies, waits for them, and re-layouts: 2.13 us -> none  [the longest x2 2.07 us: fast_body(): jnp.transpose(w, (2, 3, 0, 1, 4)).reshape(3 * ch, 9 * ch)]
    reshape x2 -> x0, local copies, waits for them, and re-layouts: 1.2 us -> none  [fast_body(): jnp.transpose(w, (2, 3, 0, 1, 4)).reshape(3 * ch, 9 * ch)]
where the time goes in v3:
time: 66.7 us; the launch traced here: 66.6 us
  Pallas kernels  64.4 us (97%)
  local copies, waits for them, and re-layouts  1.26 us (2%)
  between operations  0.67 us (1%)
    pallas_call x1, Pallas kernels, fast_body(): pl.pallas_call(block_kernel, out_shape=(jax.ShapeDtypeStruct((per_dev, ro...  64.4 us

profile of v3, /device:TPU:1, one launch (start us, length us, event | category | flops | bytes accessed | tf_op | source)
XLA Modules:
  0.0 66.6 jit_solution(868324444747946603)
XLA Ops:
  0.0 64.4 %shard_map.102 = (bf16[4,384,128]{2,1,0:T(8,128)(2,1)S(1)}, f32[8,128]{1,0:T(8,128)S(1)}) custom-call(bf16[4,384,128]{2,1,0:T(8,128)(2,1)} %bitcast.252, s32[1,64]{1,0:T(1,128)} %owner.1, s32[1,64]{1,0:T(1,128)} %slot.1, s32[1,12]{1,0:T(1,128)} %bitcast.258, f32[1,96]{1,0:T(1,128)} %bitcast.254, bf16[9,288,96]{2,1,0:T(8,128)(2,1)} %bitcast.250, ...), custom_call_target="tpu_custom_call" | custom-call | tf_op jit(solution)/shard_map/pallas_call | solution.py:479
  64.4 0.5 slice.164
  65.6 0.2 conditional.1
  65.8 0.7 %copy.175 = bf16[4,96,4,128]{3,2,1,0:T(4,128)(2,1)} copy(bf16[4,96,4,128]{3,2,1,0:T(4,128)(2,1)S(1)} %get-tuple-element.87) | data formatting | bytes 786432

commit v4 on v3

--- a/solution.py
+++ b/solution.py
@@ -187,15 +187,15 @@
     return scaled / (1.0 + jnp.exp(-scaled))
 
 
-def conv_rows(field, weights, mask, at, rows):
+def conv_rows(field, weights, mask, at, lines):
     ch, cols = field.shape[2], field.shape[3]
     right_side = jnp.concatenate(
-        [field[at : at + 3, r : r + 3].reshape(9 * ch, cols) for r in range(rows)], axis=1
+        [field[at : at + 3, r : r + 3].reshape(9 * ch, cols) for r in lines], axis=1
     )
     sums = jnp.dot(weights * mask, right_side, preferred_element_type=jnp.float32)
     lane = lax.broadcasted_iota(jnp.int32, (ch, cols), 1)
     out = []
-    for r in range(rows):
+    for r in range(len(lines)):
         part = sums[:, r * cols : (r + 1) * cols]
         low = jnp.where(lane == 0, 0.0, pltpu.roll(part[:ch], 1, 1))
         high = jnp.where(lane == cols - 1, 0.0, pltpu.roll(part[2 * ch :], cols - 1, 1))
@@ -206,7 +206,7 @@
 def block_kernel(
     groups, owner, slot, clips, gain_one, weight_one, bias_one, gain_two, weight_two, bias_two,
     out, late_out,
-    pool, sending, arrived, beside, beside_last, states, final, sched, sched_s, final_s, h_one, h_two, timeline, before, stage,
+    pool, sending, arrived, beside, beside_mid, beside_last, states, final, sched, sched_s, final_s, h_one, h_two, timeline, before, stage,
     late_all, before_final, before_final_s, raw, stacked, back,
     send_sem, recv_sem, side_send, side_recv, sched_sem, span_send, span_recv, late_send, late_recv, raw_sem,
 ):
@@ -231,6 +231,7 @@
         return pltpu.make_async_copy(sched.at[t], sched_s.at[t], sched_sem.at[0])
 
     last = per_dev + 2 * LANES * (STEPS - 1)
+    mid = last - 2 * LANES
 
     def hop(t, c, p, way):
         ends = isinstance(t, int) and t == STEPS - 1 and way == 0
@@ -243,7 +244,10 @@
 
     def side(source, entry, p):
         block = entry // (2 * LANES)
-        here = beside_last.at[entry - last] if isinstance(entry, int) and entry >= last else beside.at[entry]
+        if isinstance(entry, int) and entry >= mid:
+            here = beside_last.at[entry - last] if entry >= last else beside_mid.at[entry - mid]
+        else:
+            here = beside.at[entry]
         return pltpu.make_async_remote_copy(
             src_ref=source, dst_ref=here.at[1 - p], send_sem=side_send.at[block], recv_sem=side_recv.at[block],
             device_id=(dp, tm, sp_down if p == 0 else sp_up), device_id_type=MESH,
@@ -251,10 +255,12 @@
 
     def side_wait(block):
         every = beside.at[pl.ds(0, 2 * LANES)]
+        if isinstance(block, int) and block >= STEPS - 1:
+            here = beside_last if block == STEPS else beside_mid
+        else:
+            here = beside.at[pl.ds(2 * LANES * block, 2 * LANES)]
         pltpu.make_async_remote_copy(
-            src_ref=every, dst_ref=beside_last if isinstance(block, int) and block == STEPS else beside.at[
-                pl.ds(2 * LANES * block, 2 * LANES)
-            ],
+            src_ref=every, dst_ref=here,
             send_sem=side_send.at[block], recv_sem=side_recv.at[block],
             device_id=(dp, tm, sp_up), device_id_type=MESH,
         ).wait()
@@ -323,34 +329,61 @@
     lax.fori_loop(1, STEPS - 1, step, 0)
     final_copy = pltpu.make_async_copy(final, final_s, sched_sem.at[1])
     final_copy.start()
-    turn(STEPS - 1)
-
     final_copy.wait()
     entries = [final_s[f, tm] for f in range(2 * per_dev)]
 
+    def among(found):
+        one = two = jnp.int32(0)
+        for entry in found:
+            one = jnp.maximum(one, jnp.where((entry >= mid) & (entry < last), entry, 0))
+        for entry in found:
+            two = jnp.maximum(two, jnp.where((entry >= mid) & (entry < last) & (entry != one), entry, 0))
+        return jnp.maximum(one, mid), jnp.maximum(two, mid)
+
+    early = [jnp.where(entries[f] >= mid, 0, entries[f]) for f in range(per_dev)]
+    later = among(entries[:per_dev])
     span_copies = []
-    for j, part in enumerate((pl.ds(1, PARTS), 0, 3)):
+    for j, (at, part) in enumerate((
+        (pl.ds(0, per_dev), pl.ds(1, PARTS)), (pl.ds(per_dev, 2), pl.ds(1, PARTS)),
+        (pl.ds(0, per_dev), 0), (pl.ds(0, per_dev), 3), (pl.ds(per_dev, 2), 0), (pl.ds(per_dev, 2), 3),
+    )):
         span_copies.append(pltpu.make_async_remote_copy(
-            src_ref=stage.at[:, part], dst_ref=before.at[pl.ds(0, per_dev), part],
+            src_ref=stage.at[at, part], dst_ref=before.at[at, part],
             send_sem=span_send.at[j], recv_sem=span_recv.at[j],
             device_id=(lax.rem(dp + 1, spans), tm, sp), device_id_type=MESH,
         ))
     final_next = pltpu.make_async_remote_copy(
-        src_ref=final, dst_ref=before_final, send_sem=span_send.at[3], recv_sem=span_recv.at[3],
+        src_ref=final, dst_ref=before_final, send_sem=span_send.at[6], recv_sem=span_recv.at[6],
         device_id=(lax.rem(dp + 1, spans), tm, sp), device_id_type=MESH,
     )
 
     @pl.when(tm == 0)
     def _():
         for f in range(per_dev):
-            entry = jnp.where(entries[f] >= last, 0, entries[f])
             for p in range(PARTS):
-                stage[f, 1 + p] = pool[entry, p]
+                stage[f, 1 + p] = pool[early[f], p]
         span_copies[0].start()
         final_next.start()
 
+    turn(STEPS - 1)
+
+    @pl.when(tm == 0)
+    def _():
+        for k in range(2):
+            for p in range(PARTS):
+                stage[per_dev + k, 1 + p] = pool[later[k], p]
+        span_copies[1].start()
+        for f in range(per_dev):
+            for p in range(2):
+                stage[f, 3 * p] = beside[early[f], p]
+        span_copies[2].start()
+        span_copies[3].start()
+
     late = jnp.max(jnp.maximum(states[0], states[1]), axis=0, keepdims=True)
-    late = jnp.max(late, axis=1, keepdims=True)
+    many = ((final[:per_dev] >= mid) & (final[:per_dev] < last)).astype(jnp.int32)
+    many = jnp.sum(many, axis=0, keepdims=True) - 2
+    many = jnp.where(lax.broadcasted_iota(jnp.int32, (1, 128), 1) == 0, many, 0)
+    late = jnp.max(jnp.maximum(late, many), axis=1, keepdims=True)
     late_all[0] = jnp.broadcast_to((late > 0).astype(jnp.float32), (8, 128))
     for k in range(1, spans):
         copy = pltpu.make_async_remote_copy(
@@ -380,12 +413,11 @@
 
             @pl.when(tm == 0)
             def _():
-                for f in range(per_dev):
-                    entry = jnp.where(entries[f] >= last, 0, entries[f])
+                for k in range(2):
                     for p in range(2):
-                        stage[f, 3 * p] = beside[entry, p]
-                for copy in span_copies[1:]:
-                    copy.start()
+                        stage[per_dev + k, 3 * p] = beside_mid[later[k] - mid, p]
+                span_copies[4].start()
+                span_copies[5].start()
 
     def norm_rows(f, at, values):
         for r in range(2):
@@ -409,22 +441,33 @@
                 timeline[f - per_dev, p] = values
             norm_rows(f, 2 + 2 * p, values)
 
+    inner, outer = tuple(range(2, rows)), (0, 1, rows, rows + 1)
+
+    def first_conv(j, lines):
+        for r, act in zip(lines, conv_rows(h_one, stacked[0], masks[j], j, lines)):
+            h_two[j, r] = silu_norm(act + bias_a, gain_b).astype(jnp.bfloat16)
+
+    for j in (5, 4):
+        first_conv(j, inner)
+    others = late_all.at[pl.ds(1, spans - 1)]
+    pltpu.make_async_remote_copy(
+        src_ref=others, dst_ref=others, send_sem=late_send, recv_sem=late_recv,
+        device_id=(lax.rem(dp + 1, spans), tm, sp), device_id_type=MESH,
+    ).wait()
+    late_out[...] = jnp.max(late_all[...], axis=0).astype(jnp.int32)
     side_wait(STEPS)
 
     for k in range(2 * LANES):
         for p in range(2):
+            beside[mid + k, p] = beside_mid[k, p]
             beside[last + k, p] = beside_last[k, p]
     for f in range(2 * per_dev):
         for p in range(2):
             norm_rows(f, 6 * p, beside[entries[f], p])
     outside(h_one, 2, rows + 2)
 
-    def first_conv(j):
-        for r, act in enumerate(conv_rows(h_one, stacked[0], masks[j], j, rows + 2)):
-            h_two[j, r] = silu_norm(act + bias_a, gain_b).astype(jnp.bfloat16)
-
-    first_conv(5)
-    first_conv(4)
+    first_conv(5, outer)
+    first_conv(4, outer)
 
     @pl.when(tm == 0)
     def _():
@@ -433,38 +476,34 @@
         move.start()
         for c in range(LANES):
             for p in range(2):
-                before[per_dev + c, 1 + p] = pool[last + c, p]
-                before[per_dev + c, 3 * p] = beside_last[c, p]
+                before[per_dev + 2 + c, 1 + p] = pool[last + c, p]
+                before[per_dev + 2 + c, 3 * p] = beside_last[c, p]
         for copy in span_copies:
             copy.wait()
         move.wait()
+        found = [before_final_s[f, 0] for f in range(per_dev)]
+        one, _ = among(found)
         for f in range(per_dev):
-            entry = before_final_s[f, 0]
-            entry = jnp.where(entry >= last, per_dev + jnp.minimum(entry - last, LANES - 1), f)
+            entry = jnp.where(found[f] == one, per_dev, per_dev + 1)
+            entry = jnp.where(found[f] >= mid, entry, f)
+            entry = jnp.where(found[f] >= last, per_dev + 2 + jnp.minimum(found[f] - last, LANES - 1), entry)
             for q in range(4):
                 norm_rows(f, 2 * q, before[entry, q])
         outside(h_one, 2, rows + 2)
 
     for j in (3, 2, 1, 0):
-        first_conv(j)
+        first_conv(j, range(rows + 2))
     outside(h_two, 1, rows + 1)
     for pair in ((3, 2), (1, 0)):
         ready = []
         for s in pair:
-            mixed = jnp.concatenate(conv_rows(h_two, stacked[1], masks[s + 2], s, rows), axis=0)
+            mixed = jnp.concatenate(conv_rows(h_two, stacked[1], masks[s + 2], s, range(rows)), axis=0)
             kept = timeline[s].reshape(size, cols).astype(jnp.float32)
             bias = jnp.concatenate([bias_b] * rows, axis=0)
             ready.append((kept + mixed + bias).astype(jnp.bfloat16))
         turned = jnp.dot(back[...], jnp.concatenate(ready, axis=1), preferred_element_type=jnp.float32)
         for k, s in enumerate(pair):
             out[s] = turned[:, k * cols : (k + 1) * cols].astype(jnp.bfloat16)
-
-    others = late_all.at[pl.ds(1, spans - 1)]
-    pltpu.make_async_remote_copy(
-        src_ref=others, dst_ref=others, send_sem=late_send, recv_sem=late_recv,
-        device_id=(lax.rem(dp + 1, spans), tm, sp), device_id_type=MESH,
-    ).wait()
-    late_out[...] = jnp.max(late_all[...], axis=0)
 
 
 def fast_body(
@@ -480,7 +519,7 @@
         block_kernel,
         out_shape=(
             jax.ShapeDtypeStruct((per_dev, rows * ch, cols), jnp.bfloat16),
-            jax.ShapeDtypeStruct((8, 128), jnp.float32),
+            jax.ShapeDtypeStruct((8, 128), jnp.int32),
         ),
         in_specs=[vmem, vmem, vmem, smem, vmem, whole, vmem, vmem, whole, vmem],
         out_specs=(vmem, vmem),
@@ -490,6 +529,7 @@
             pltpu.VMEM((STEPS * LANES, PARTS, 2) + part[1:], jnp.bfloat16),
             pltpu.VMEM((per_dev + sends,) + part, jnp.bfloat16),
             pltpu.VMEM((2 * LANES,) + part, jnp.bfloat16),
+            pltpu.VMEM((2 * LANES,) + part, jnp.bfloat16),
             pltpu.VMEM((2, plan_owner.shape[1], 128), jnp.int32),
             pltpu.VMEM((8, 128), jnp.int32),
             pltpu.VMEM((STEPS, 8, 128), jnp.int32),
@@ -498,8 +538,8 @@
             pltpu.VMEM((2 * per_dev, rows + 4, ch, cols), jnp.bfloat16),
             pltpu.VMEM((per_dev + 2, rows + 2, ch, cols), jnp.bfloat16),
             pltpu.VMEM((per_dev,) + part, jnp.bfloat16),
-            pltpu.VMEM((per_dev + LANES, 4) + part[1:], jnp.bfloat16),
-            pltpu.VMEM((per_dev, 4) + part[1:], jnp.bfloat16),
+            pltpu.VMEM((per_dev + 2 + LANES, 4) + part[1:], jnp.bfloat16),
+            pltpu.VMEM((per_dev + 2, 4) + part[1:], jnp.bfloat16),
             pltpu.VMEM((spans, 8, 128), jnp.float32),
             pltpu.VMEM((8, 128), jnp.int32),
             pltpu.SMEM((8, 128), jnp.int32),
@@ -511,8 +551,8 @@
             pltpu.SemaphoreType.DMA((STEPS + 1,)),
             pltpu.SemaphoreType.DMA((STEPS + 1,)),
             pltpu.SemaphoreType.DMA((2,)),
-            pltpu.SemaphoreType.DMA((4,)),
-            pltpu.SemaphoreType.DMA((4,)),
+            pltpu.SemaphoreType.DMA((7,)),
+            pltpu.SemaphoreType.DMA((7,)),
             pltpu.SemaphoreType.DMA,
             pltpu.SemaphoreType.DMA,
             pltpu.SemaphoreType.DMA((2,)),
@@ -529,10 +569,9 @@
 
 def body(*args):
     fast, late = fast_body(*args)
-    return lax.cond(
-        late[0, 0] > 0,
-        lambda *args: general_body(*args),
-        lambda *args: fast.reshape(args[0].shape[:1] + args[0].shape[2:]),
+    return lax.switch(
+        late[0, 0],
+        (lambda *args: fast.reshape(args[0].shape[:1] + args[0].shape[2:]), lambda *args: general_body(*args)),
         *args,
     )
 

time: 66.7 us -> 69.2 us (1.037)
  Pallas kernels: 64.4 us -> 66.9 us
    pallas_call x1, Pallas kernels: 64.4 us -> 66.9 us  [fast_body(): pl.pallas_call(block_kernel, out_shape=(jax.ShapeDtypeStruct((per_dev, ro...]
where the time goes in v4:
time: 69.2 us; the launch traced here: 69.1 us
  Pallas kernels  66.9 us (97%)
  local copies, waits for them, and re-layouts  1.26 us (2%)
    pallas_call x1, Pallas kernels, fast_body(): pl.pallas_call(block_kernel, out_shape=(jax.ShapeDtypeStruct((per_dev, ro...  66.9 us

profile of v4, /device:TPU:1, one launch (start us, length us, event | category | flops | bytes accessed | tf_op | source)
XLA Modules:
  0.0 69.1 jit_solution(2372696373509103594)
XLA Ops:
  0.0 66.9 %shard_map.102 = (bf16[4,384,128]{2,1,0:T(8,128)(2,1)S(1)}, s32[8,128]{1,0:T(8,128)S(1)}) custom-call(bf16[4,384,128]{2,1,0:T(8,128)(2,1)} %bitcast.252, s32[1,64]{1,0:T(1,128)} %owner.1, s32[1,64]{1,0:T(1,128)} %slot.1, s32[1,12]{1,0:T(1,128)} %bitcast.258, f32[1,96]{1,0:T(1,128)} %bitcast.254, bf16[9,288,96]{2,1,0:T(8,128)(2,1)} %bitcast.250, ...), custom_call_target="tpu_custom_call" | custom-call | tf_op jit(solution)/shard_map/pallas_call | solution.py:518
  66.9 0.5 slice.164
  68.1 0.2 conditional.1
  68.3 0.7 %copy.175 = bf16[4,96,4,128]{3,2,1,0:T(4,128)(2,1)} copy(bf16[4,96,4,128]{3,2,1,0:T(4,128)(2,1)S(1)} %get-tuple-element.87) | data formatting | bytes 786432

commit v5 on v3

--- a/solution.py
+++ b/solution.py
@@ -187,15 +187,15 @@
     return scaled / (1.0 + jnp.exp(-scaled))
 
 
-def conv_rows(field, weights, mask, at, rows):
+def conv_rows(field, weights, mask, at, lines):
     ch, cols = field.shape[2], field.shape[3]
     right_side = jnp.concatenate(
-        [field[at : at + 3, r : r + 3].reshape(9 * ch, cols) for r in range(rows)], axis=1
+        [field[at : at + 3, r : r + 3].reshape(9 * ch, cols) for r in lines], axis=1
     )
     sums = jnp.dot(weights * mask, right_side, preferred_element_type=jnp.float32)
     lane = lax.broadcasted_iota(jnp.int32, (ch, cols), 1)
     out = []
-    for r in range(rows):
+    for r in range(len(lines)):
         part = sums[:, r * cols : (r + 1) * cols]
         low = jnp.where(lane == 0, 0.0, pltpu.roll(part[:ch], 1, 1))
         high = jnp.where(lane == cols - 1, 0.0, pltpu.roll(part[2 * ch :], cols - 1, 1))
@@ -409,6 +409,20 @@
                 timeline[f - per_dev, p] = values
             norm_rows(f, 2 + 2 * p, values)
 
+    inner, outer = tuple(range(2, rows)), (0, 1, rows, rows + 1)
+
+    def first_conv(j, lines):
+        for r, act in zip(lines, conv_rows(h_one, stacked[0], masks[j], j, lines)):
+            h_two[j, r] = silu_norm(act + bias_a, gain_b).astype(jnp.bfloat16)
+
+    for j in (5, 4):
+        first_conv(j, inner)
+    others = late_all.at[pl.ds(1, spans - 1)]
+    pltpu.make_async_remote_copy(
+        src_ref=others, dst_ref=others, send_sem=late_send, recv_sem=late_recv,
+        device_id=(lax.rem(dp + 1, spans), tm, sp), device_id_type=MESH,
+    ).wait()
+    late_out[...] = jnp.max(late_all[...], axis=0).astype(jnp.int32)
     side_wait(STEPS)
 
     for k in range(2 * LANES):
@@ -419,12 +433,8 @@
             norm_rows(f, 6 * p, beside[entries[f], p])
     outside(h_one, 2, rows + 2)
 
-    def first_conv(j):
-        for r, act in enumerate(conv_rows(h_one, stacked[0], masks[j], j, rows + 2)):
-            h_two[j, r] = silu_norm(act + bias_a, gain_b).astype(jnp.bfloat16)
-
-    first_conv(5)
-    first_conv(4)
+    first_conv(5, outer)
+    first_conv(4, outer)
 
     @pl.when(tm == 0)
     def _():
@@ -446,25 +456,18 @@
         outside(h_one, 2, rows + 2)
 
     for j in (3, 2, 1, 0):
-        first_conv(j)
+        first_conv(j, range(rows + 2))
     outside(h_two, 1, rows + 1)
     for pair in ((3, 2), (1, 0)):
         ready = []
         for s in pair:
-            mixed = jnp.concatenate(conv_rows(h_two, stacked[1], masks[s + 2], s, rows), axis=0)
+            mixed = jnp.concatenate(conv_rows(h_two, stacked[1], masks[s + 2], s, range(rows)), axis=0)
             kept = timeline[s].reshape(size, cols).astype(jnp.float32)
             bias = jnp.concatenate([bias_b] * rows, axis=0)
             ready.append((kept + mixed + bias).astype(jnp.bfloat16))
         turned = jnp.dot(back[...], jnp.concatenate(ready, axis=1), preferred_element_type=jnp.float32)
         for k, s in enumerate(pair):
             out[s] = turned[:, k * cols : (k + 1) * cols].astype(jnp.bfloat16)
-
-    others = late_all.at[pl.ds(1, spans - 1)]
-    pltpu.make_async_remote_copy(
-        src_ref=others, dst_ref=others, send_sem=late_send, recv_sem=late_recv,
-        device_id=(lax.rem(dp + 1, spans), tm, sp), device_id_type=MESH,
-    ).wait()
-    late_out[...] = jnp.max(late_all[...], axis=0)
 
 
 def fast_body(
@@ -480,7 +483,7 @@
         block_kernel,
         out_shape=(
             jax.ShapeDtypeStruct((per_dev, rows * ch, cols), jnp.bfloat16),
-            jax.ShapeDtypeStruct((8, 128), jnp.float32),
+            jax.ShapeDtypeStruct((8, 128), jnp.int32),
         ),
         in_specs=[vmem, vmem, vmem, smem, vmem, whole, vmem, vmem, whole, vmem],
         out_specs=(vmem, vmem),
@@ -529,10 +532,9 @@
 
 def body(*args):
     fast, late = fast_body(*args)
-    return lax.cond(
-        late[0, 0] > 0,
-        lambda *args: general_body(*args),
-        lambda *args: fast.reshape(args[0].shape[:1] + args[0].shape[2:]),
+    return lax.switch(
+        late[0, 0],
+        (lambda *args: fast.reshape(args[0].shape[:1] + args[0].shape[2:]), lambda *args: general_body(*args)),
         *args,
     )
 

time: 66.7 us -> 66.4 us (level)
  no operation moved by 1% of the time
where the time goes in v5:
time: 66.4 us; the launch traced here: 66.3 us
  Pallas kernels  64.1 us (97%)
  local copies, waits for them, and re-layouts  1.26 us (2%)
  between operations  0.67 us (1%)
    pallas_call x1, Pallas kernels, fast_body(): pl.pallas_call(block_kernel, out_shape=(jax.ShapeDtypeStruct((per_dev, ro...  64.1 us

profile of v5, /device:TPU:1, one launch (start us, length us, event | category | flops | bytes accessed | tf_op | source)
XLA Modules:
  0.0 66.3 jit_solution(12828313220265653519)
XLA Ops:
  0.0 64.1 %shard_map.102 = (bf16[4,384,128]{2,1,0:T(8,128)(2,1)S(1)}, s32[8,128]{1,0:T(8,128)S(1)}) custom-call(bf16[4,384,128]{2,1,0:T(8,128)(2,1)} %bitcast.252, s32[1,64]{1,0:T(1,128)} %owner.1, s32[1,64]{1,0:T(1,128)} %slot.1, s32[1,12]{1,0:T(1,128)} %bitcast.258, f32[1,96]{1,0:T(1,128)} %bitcast.254, bf16[9,288,96]{2,1,0:T(8,128)(2,1)} %bitcast.250, ...), custom_call_target="tpu_custom_call" | custom-call | tf_op jit(solution)/shard_map/pallas_call | solution.py:482
  64.1 0.5 slice.164
  65.3 0.2 conditional.1
  65.5 0.7 %copy.175 = bf16[4,96,4,128]{3,2,1,0:T(4,128)(2,1)} copy(bf16[4,96,4,128]{3,2,1,0:T(4,128)(2,1)S(1)} %get-tuple-element.87) | data formatting | bytes 786432
